TPU v7x, 32 devices: a whole 2x2x4 slice. The times are simulated.
32 devices in a mesh: branch: 2 (over core), tp: 4 (over y, x), seq: 4 (over z).
Axes of the slice: x: 2, y: 2, z: 4, core: 2. Of those that a mesh axis runs over, the one named last changes fastest.
Arguments:
- block_input: bfloat16 [8, 2048, 2048], P('seq', 'tp'), may hold values from -6 to 6
- first_norm_gain: bfloat16 [2048], replicated, may hold values from 0.25 to 1.75
- first_norm_bias: bfloat16 [2048], replicated, may hold values from -1.5 to 1.5
- second_norm_gain: bfloat16 [2048], replicated, may hold values from 0.25 to 1.75
- second_norm_bias: bfloat16 [2048], replicated, may hold values from -1.5 to 1.5
- query_key_value: bfloat16 [2048, 6144], P(('branch', 'seq'), 'tp'), may hold values from -0.125 to 0.125
- query_key_value_bias: bfloat16 [6144], P('tp'), may hold values from -1.5 to 1.5
- attention_dense: bfloat16 [2048, 2048], P('tp', ('branch', 'seq')), may hold values from -0.375 to 0.375
- attention_dense_bias: bfloat16 [2048], replicated, may hold values from -1.5 to 1.5
- expand_weight: bfloat16 [2048, 8192], P(('branch', 'seq'), 'tp'), may hold values from -0.125 to 0.125
- expand_bias: bfloat16 [8192], P('tp'), may hold values from -2.5 to 2.5
- contract_weight: bfloat16 [8192, 2048], P('tp', ('branch', 'seq')), may hold values from -0.09375 to 0.09375
- contract_bias: bfloat16 [2048], replicated, may hold values from -1.5 to 1.5
- document_starts: int32 [8, 8], P('seq'), may hold values from 0 to 2048, as said below
- output_grad: bfloat16 [8, 2048, 2048], P('seq', 'tp'), may hold values from -6 to 6
Outputs:
- block_output: bfloat16 [8, 2048, 2048], P('seq', 'tp')
- input_grad: bfloat16 [8, 2048, 2048], P('seq', 'tp')
- first_gain_grad: float32 [2048], replicated
- first_bias_grad: float32 [2048], replicated
- second_gain_grad: float32 [2048], replicated
- second_bias_grad: float32 [2048], replicated
- query_key_value_grad: float32 [2048, 6144], P(('branch', 'seq'), 'tp')
- query_key_value_bias_grad: float32 [6144], P('tp')
- dense_grad: float32 [2048, 2048], P('tp', ('branch', 'seq'))
- dense_bias_grad: float32 [2048], replicated
- expand_grad: float32 [2048, 8192], P(('branch', 'seq'), 'tp')
- expand_bias_grad: float32 [8192], P('tp')
- contract_grad: float32 [8192, 2048], P('tp', ('branch', 'seq'))
- contract_bias_grad: float32 [2048], replicated
Inputs may be any that keep to these rules, and one draw needn't show every extreme that they name: `document_starts`: each row lists where the documents of one packed sequence begin: it starts with 0, rises strictly, and the entries after its last document are 2048. Among the 2 rows of each index of seq, one (drawn) has a document that begins before position 512 and ends after position 1536; the others hold 2 to 8 documents.
All inputs are finite; a program needn't handle non-finite values.
Results may differ from a plain program's by a relative error of at most 0.01.
Values may be sent and summed in bfloat16 or wider, within the bound.
No kernel may reach another device: no remote copies, remote signals or barrier semaphores. Data moves between devices by JAX's collectives and lax.ppermute only.
A program may use at most 704 MiB of HBM per device.

v0:
```python
from functools import partial
import math

import jax
import jax.numpy as jnp
from jax import lax
from jax.experimental import pallas as pl
from jax.experimental.pallas import tpu as pltpu
from jax.sharding import PartitionSpec as P

HD = 128
ROT = 32


EPSILON = 1e-05
NEGATIVE = -1e30
ROPE_BASE = 10000.0
LOG2E = math.log2(math.e)
F32 = jnp.float32
BF16 = jnp.bfloat16
CONTRACT_LAST = (((1,), (1,)), ((), ()))
CONTRACT_FIRST = (((0,), (0,)), ((), ()))
VMEM_BYTES = 56 * 1024 * 1024
ANY = pl.BlockSpec(memory_space=pl.ANY)
HINT = 0.02


def cost(flops, moved, transcendentals=0):
    return pl.CostEstimate(
        flops=1 + int(flops * HINT), bytes_accessed=1 + int(moved * HINT), transcendentals=0
    )


def launch(
    kernel,
    operands,
    in_specs,
    grid,
    out_specs,
    out_shape,
    name,
    cost_estimate,
    prefetch=(),
    held=(),
    tokens=(),
    scratch_shapes=(),
):
    lead = len(prefetch) + len(operands)
    extra = len(held) + len(tokens)

    def body(*refs):
        kernel(*refs[:lead], *refs[lead + extra :])

    return pl.pallas_call(
        body,
        grid_spec=pltpu.PrefetchScalarGridSpec(
            num_scalar_prefetch=len(prefetch),
            grid=grid,
            in_specs=list(in_specs) + [ANY] * extra,
            out_specs=out_specs,
            scratch_shapes=list(scratch_shapes),
        ),
        out_shape=out_shape,
        input_output_aliases={lead + k: k for k in range(len(held))},
        compiler_params=pltpu.CompilerParams(
            dimension_semantics=("arbitrary",) * len(grid), vmem_limit_bytes=VMEM_BYTES
        ),
        cost_estimate=cost_estimate,
        name=name,
    )(*prefetch, *operands, *held, *tokens)


def hold(value, *tokens):
    def nothing(out):
        pass

    return launch(
        nothing,
        [],
        [],
        (1,),
        ANY,
        jax.ShapeDtypeStruct(value.shape, value.dtype),
        "hold",
        cost(1, 1),
        held=[value],
        tokens=tokens,
    )


def swap(value, axis, bit):
    size = lax.axis_size(axis)
    return lax.ppermute(value, axis, [(i, i ^ bit) for i in range(size)])


def onward(value, axis):
    size = lax.axis_size(axis)
    return lax.ppermute(value, axis, [(i, (i + 1) % size) for i in range(size)])


def bit_orders(size):
    bits = [1 << k for k in range(size.bit_length() - 1)]
    return (bits, bits[::-1])


def last_bit(number, order):
    return [bit for bit in order if number & bit][-1]


def gather_near(own, number):
    size = lax.axis_size("tp")
    bits = [1 << k for k in range(size.bit_length() - 1)]
    return {
        (bit, (n + number) % 2): swap(own[(n + number) % 2], "tp", bit)
        for n, bit in enumerate(bits)
    }


def hold_all(items, *tokens):
    return {key: hold(item, *tokens) for key, item in items.items()}


def in_pieces(first, second):
    items = {**first, **second}
    return {j: [items[j, 0], items[j, 1]] for j in sorted({j for j, _ in items})}


def gather_far(near):
    size = lax.axis_size("tp")
    pieces = dict(near)
    far = {}
    for j in sorted(range(1, size), key=lambda j: bin(j).count("1")):
        if j not in near:
            bits = [last_bit(j, order) for order in bit_orders(size)]
            far[j] = [swap(pieces[j ^ bit][q], "tp", bit) for q, bit in enumerate(bits)]
            pieces[j] = far[j]
    return far


def with_other_core(items):
    return items + [swap(item, "branch", 1) for item in items]


def add_up(items):
    total = items[0].astype(F32)
    for item in items[1:]:
        total = total + item.astype(F32)
    return total


class TileSum:
    def __init__(self):
        size = lax.axis_size("tp")
        self.orders = bit_orders(size)
        self.waiting = [(q, j) for j in range(1, size) for q in range(2)]
        self.expected = {(q, j): 0 for j in range(size) for q in range(2)}
        for q, j in self.waiting:
            self.expected[q, j ^ last_bit(j, self.orders[q])] += 1
        self.waiting.sort(key=lambda at: (-bin(at[1]).count("1"), at[1]))
        self.pieces = {}
        self.arrived = {}
        self.moving = []

    def splits(self, j):
        return j > 0 and len({last_bit(j, order) for order in self.orders}) > 1

    def extras(self, j):
        return [(q, item) for q in range(2) for item in self.arrived.get((q, j), [])]

    def complete(self, j):
        return all(len(self.arrived.get((q, j), [])) == self.expected[q, j] for q in range(2))

    def send(self, *tokens):
        operands = []
        for q, j in list(self.waiting):
            if j not in self.pieces or (q, j) not in self.waiting:
                continue
            bit = last_bit(j, self.orders[q])
            if self.splits(j):
                sides, operand = [q], self.pieces[j][q]
            else:
                sides, operand = [0, 1], self.pieces[j]
            for side in sides:
                self.waiting.remove((side, j))
            if tokens:
                operand = hold(operand, *tokens)
            self.moving.append((sides, j ^ bit, swap(operand, "tp", bit)))
            operands.append(operand)
        return operands

    def land(self, *tokens):
        items = []
        for sides, j, item in self.moving:
            item = hold(item, *tokens) if tokens else item
            items.append(item)
            if j == 0:
                self.arrived.setdefault(0, []).append(item)
                continue
            half = item.shape[0] // 2
            for side in sides:
                part = item[side * half : (side + 1) * half] if len(sides) > 1 else item
                self.arrived.setdefault((side, j), []).append(part)
        self.moving = []
        return items

    def terms(self):
        return [[(item, 0), (item, 1)] for item in [self.pieces[0]] + self.arrived[0]]


def finish_piece(total, column, extras, outs):
    half = total.shape[0] // 2
    width = total.shape[1]
    cols = slice(column, column + width)
    parts = [total[:half], total[half:]]
    for q, ref in extras:
        parts[q] = parts[q] + ref[:, cols].astype(F32)
    for q in range(2):
        if len(outs) > 1:
            outs[q][:, cols] = parts[q].astype(BF16)
        else:
            outs[0][q * half : (q + 1) * half, cols] = parts[q].astype(BF16)


def piece_specs(tile, share, steps, split):
    rows, count = (tile // 2, 2) if split else (tile, 1)
    return (
        [pl.BlockSpec((rows, share), lambda i: (0, i))] * count,
        [jax.ShapeDtypeStruct((rows, steps * share), BF16)] * count,
    )


def all_sum(value, axis):
    size = lax.axis_size(axis)
    bit = 1
    while bit < size:
        value = value + swap(value, axis, bit)
        bit *= 2
    return value


def rope(vectors, cosine, sine_up, sine_down):
    return (
        vectors * cosine
        + pltpu.roll(vectors, ROT // 2, 1) * sine_up
        + pltpu.roll(vectors, HD - ROT // 2, 1) * sine_down
    )


class Documents:
    def __init__(self, place, starts, seq_at, rows):
        self.row = place[1] ^ seq_at
        self.starts = starts
        self.rows = rows

    def begin(self, places):
        begin = jnp.zeros_like(places)
        for number in range(self.starts.shape[1]):
            start = self.starts[self.row, number]
            begin = jnp.where(places >= start, start, begin)
        return begin

    def first_key_block(self, block):
        return lax.div(self.begin(block * self.rows), jnp.int32(self.rows))

    def last_query_block(self, block, blocks):
        last = block
        for number in range(1, blocks):
            after = jnp.minimum(block + number, blocks - 1)
            last = jnp.where(self.first_key_block(after) <= block, jnp.maximum(last, after), last)
        return last


def table_kernel(place, starts, cosine, sine_up, sine_down):
    rows = cosine.shape[0]
    blocks = lax.axis_size("tp")
    step = pl.program_id(0)
    block, seq_at = lax.rem(step, blocks) ^ place[0], lax.div(step, blocks)
    places = block * rows + lax.broadcasted_iota(jnp.int32, (rows, 1), 0)
    begin = Documents(place, starts, seq_at, rows).begin(places)
    lane = lax.broadcasted_iota(jnp.int32, (1, HD), 1)
    half = ROT // 2
    number = jnp.where(lane < half, lane, lane - half).astype(F32)
    frequency = jnp.exp2(number * (-2.0 / ROT * math.log2(ROPE_BASE)))
    angles = (places - begin).astype(F32) * jnp.where(lane < ROT, frequency, 0.0)
    cosine[...] = jnp.cos(angles)
    sines = jnp.sin(angles)
    sine_up[...] = jnp.where((lane >= half) & (lane < ROT), sines, 0.0)
    sine_down[...] = jnp.where(lane < half, -sines, 0.0)


def rotary_tables(place, starts, rows, tokens):
    steps = 2 * lax.axis_size("tp")
    tile = rows // steps
    out = pl.BlockSpec((tile, HD), lambda i, *_: (i, 0))
    return launch(
        table_kernel,
        [],
        [],
        (steps,),
        [out] * 3,
        [jax.ShapeDtypeStruct((rows, HD), F32)] * 3,
        "rotary_tables",
        cost(rows * HD * 100, rows * HD * 48),
        prefetch=[place, starts],
        tokens=tokens,
    )


def half_of_piece(j):
    size = lax.axis_size("tp")
    return lambda i, *_: ((lax.div(i, 2) * size + j) * 2 + lax.rem(i, 2), 0)


def own_tile_specs(tile):
    _, rows, width = tile.shape

    def spec(h, q):
        return pl.BlockSpec((1, rows // 2, width), lambda i, place: (place[1] ^ h, q, 0))

    return [spec(h, q) for h in range(2) for q in range(2)]


def own_halves(place, tile, tokens=()):
    _, rows, width = tile.shape

    def kernel(place, first, second, out_first, out_second):
        out_first[...] = first[0]
        out_second[...] = second[0]

    shape = jax.ShapeDtypeStruct((rows // 2, width), BF16)
    return launch(
        kernel,
        [tile, tile],
        own_tile_specs(tile)[:2],
        (1,),
        [whole_spec(shape)] * 2,
        [shape, shape],
        "own_halves",
        cost(1, 4 * rows * width),
        prefetch=[place],
        tokens=tokens,
    )


def place_kernel(place, x0, x1, x2, x3, out):
    step = pl.program_id(0)
    for number, x_ref in enumerate((x0, x1, x2, x3)):

        @pl.when(step == number)
        def _(x_ref=x_ref):
            out[...] = x_ref[...].reshape(out.shape)


def place_piece(j, place, halves, rows_in_all, held, tokens=()):
    if j == 0:
        specs = own_tile_specs(halves)
        half, model_width = halves.shape[1] // 2, halves.shape[2]
        halves = [halves] * 4
    else:
        half, model_width = halves[0].shape
        specs = [whole_spec(item) for item in halves]
    return launch(
        place_kernel,
        halves,
        specs,
        (4,),
        pl.BlockSpec((half, model_width), half_of_piece(j)),
        jax.ShapeDtypeStruct((rows_in_all, model_width), BF16),
        "place_piece",
        cost(1, 4 * half * model_width * 4),
        prefetch=[place],
        held=held,
        tokens=tokens,
    )


def norm_kernel(place, x0, x1, x2, x3, gain1, shift1, gain2, shift2, *rest):
    normal, first, second, mark, scratch = rest[-5:]
    step = pl.program_id(0)
    mark[...] = jnp.zeros_like(mark)
    for number, x_ref in enumerate((x0, x1, x2, x3)):

        @pl.when(step == number)
        def _(x_ref=x_ref):
            scratch[...] = (x_ref[0] if len(x_ref.shape) == 3 else x_ref[...]).astype(F32)

    x = scratch[...]
    centred = x - jnp.mean(x, axis=-1, keepdims=True)
    variance = jnp.mean(centred * centred, axis=-1, keepdims=True)
    n = centred * lax.rsqrt(variance + EPSILON)
    normal[...] = n.astype(BF16)
    first[...] = (n * gain1[...] + shift1[...]).astype(BF16)
    second[...] = (n * gain2[...] + shift2[...]).astype(BF16)


def norm_piece(j, place, halves, rows_in_all, gains, held, tokens):
    if j == 0:
        specs = own_tile_specs(halves)
        half, model_width = halves.shape[1] // 2, halves.shape[2]
        halves = [halves] * 4
    else:
        half, model_width = halves[0].shape
        specs = [whole_spec(item) for item in halves]
    wide = pl.BlockSpec((half, model_width), half_of_piece(j))
    return launch(
        norm_kernel,
        halves + list(gains),
        specs + [whole_spec(item) for item in gains],
        (4,),
        [wide] * 3 + [pl.BlockSpec((8, HD), lambda i, *_: (0, 0))],
        [jax.ShapeDtypeStruct((rows_in_all, model_width), BF16)] * 3
        + [jax.ShapeDtypeStruct((8, HD), F32)],
        "norm_piece",
        cost(4 * half * model_width * 16, 4 * half * model_width * 16),
        prefetch=[place],
        held=held,
        tokens=tokens,
        scratch_shapes=[pltpu.VMEM((half, model_width), F32)],
    )


def chunks_of(weight):
    groups, cores = weight.shape[:2]
    return [(z, c, c * groups + z) for c in range(cores) for z in range(groups)]


def row_product(left, weight, share):
    total = None
    for z, c, at in chunks_of(weight):
        part = jnp.dot(
            left[:, at * share : (at + 1) * share], weight[z, c], preferred_element_type=F32
        )
        total = part if total is None else total + part
    return total


def column_back(left, weight, share):
    total = None
    for z, c, at in chunks_of(weight):
        part = lax.dot_general(
            left[:, at * share : (at + 1) * share],
            weight[z, c],
            CONTRACT_LAST,
            preferred_element_type=F32,
        )
        total = part if total is None else total + part
    return total


def whole_spec(array, prefetched=0):
    rank = array.ndim
    return pl.BlockSpec(array.shape, lambda *at: (0,) * rank)


def project_kernel(normed, weight, bias, cosine, sine_up, sine_down, queries, keys, values):
    joined = row_product(normed, weight, weight.shape[2]) + bias[...]
    tables = (cosine[...], sine_up[...], sine_down[...])
    for head in range(queries.shape[0]):
        at = head * 3 * HD
        queries[head, 0, 0] = rope(joined[:, at : at + HD], *tables).astype(BF16)
        keys[head, 0, 0] = rope(joined[:, at + HD : at + 2 * HD], *tables).astype(BF16)
        values[head, 0, 0] = joined[:, at + 2 * HD : at + 3 * HD].astype(BF16)


def project(first, last, normed, weight, bias, tables, held):
    rows, model_width = normed.shape
    joined_cols = weight.shape[3]
    heads = joined_cols // (3 * HD)
    size = lax.axis_size("tp")
    tile = rows // (2 * size)
    table = pl.BlockSpec((tile, HD), lambda s, i: (s * size + first + i, 0))
    share = (last - first) / size
    return launch(
        project_kernel,
        [normed, weight, bias] + list(tables),
        [
            pl.BlockSpec((tile, model_width), lambda s, i: (s * size + first + i, 0)),
            whole_spec(weight),
            whole_spec(bias),
            table,
            table,
            table,
        ],
        (2, last - first),
        [pl.BlockSpec((heads, 1, 1, tile, HD), lambda s, i: (0, s, first + i, 0, 0))] * 3,
        [jax.ShapeDtypeStruct((heads, 2, size, tile, HD), BF16)] * 3,
        "project",
        cost(
            2 * rows * share * model_width * joined_cols,
            2 * (rows * share * (model_width + joined_cols) + weight.size),
        ),
        held=held,
    )


def attend_kernel(place, starts, q_ref, k_ref, v_ref, out_ref, send_ref, lse_ref):
    block = pl.program_id(1)
    heads, rows = q_ref.shape[0], q_ref.shape[-2]
    here = place[0]
    documents = Documents(place, starts, pl.program_id(0), rows)
    low = documents.first_key_block(block)
    query_places = block * rows + lax.broadcasted_iota(jnp.int32, (rows, 1), 0)
    begin = documents.begin(query_places)
    factor = LOG2E / math.sqrt(HD)

    def step(number, carry):
        key_places = number * rows + lax.broadcasted_iota(jnp.int32, (1, rows), 1)
        allowed = (key_places >= begin) & (key_places <= query_places)
        results = []
        for head in range(heads):
            top, total, mixed = carry[head]
            key = k_ref[head, 0, number ^ here]
            value = v_ref[head, 0, number ^ here]
            scores = lax.dot_general(
                q_ref[head, 0, 0], key, CONTRACT_LAST, preferred_element_type=F32
            )
            scores = jnp.where(allowed, scores * factor, NEGATIVE)
            new_top = jnp.maximum(top, jnp.max(scores, axis=-1, keepdims=True))
            weights = jnp.exp2(scores - new_top)
            shrink = jnp.exp2(top - new_top)
            total = total * shrink + jnp.sum(weights, axis=-1, keepdims=True)
            mixed = mixed * shrink + jnp.dot(
                weights.astype(BF16), value, preferred_element_type=F32
            )
            results.append((new_top, total, mixed))
        return tuple(results)

    empty = (
        jnp.full((rows, 1), NEGATIVE, F32),
        jnp.zeros((rows, 1), F32),
        jnp.zeros((rows, HD), F32),
    )
    results = lax.fori_loop(low, block + 1, step, (empty,) * heads)
    for head, (top, total, mixed) in enumerate(results):
        result = (mixed / total).astype(BF16)
        out_ref[0, 0, :, head * HD : (head + 1) * HD] = result
        send_ref[0, :, head * HD : (head + 1) * HD] = result
        log_sum = top + jnp.log(total) * LOG2E
        lse_ref[head, 0, 0] = jnp.broadcast_to(log_sum, (rows, HD)).T[:1]


def attend(place, starts, queries, keys, values, tokens):
    heads, seqs, blocks, rows, _ = queries.shape
    one = pl.BlockSpec(
        (heads, 1, 1, rows, HD), lambda s, i, place, starts: (0, s, i ^ place[0], 0, 0)
    )
    full = pl.BlockSpec((heads, 1, blocks, rows, HD), lambda s, i, *_: (0, s, 0, 0, 0))
    pairs = heads * seqs * blocks * (blocks + 1) // 2
    return launch(
        attend_kernel,
        [queries, keys, values],
        [one, full, full],
        (seqs, blocks),
        [
            pl.BlockSpec(
                (1, 1, rows, heads * HD), lambda s, i, place, starts: (s, i ^ place[0], 0, 0)
            ),
            pl.BlockSpec(
                (1, rows, heads * HD), lambda s, i, place, starts: ((s * i) ^ place[0], 0, 0)
            ),
            pl.BlockSpec(
                (heads, 1, 1, 1, rows), lambda s, i, place, starts: (0, s, i ^ place[0], 0, 0)
            ),
        ],
        [
            jax.ShapeDtypeStruct((seqs, blocks, rows, heads * HD), BF16),
            jax.ShapeDtypeStruct((blocks, rows, heads * HD), BF16),
            jax.ShapeDtypeStruct((heads, seqs, blocks, 1, rows), F32),
        ],
        "attend",
        cost(pairs * 30 * rows * rows * HD, 4 * queries.size * 2),
        prefetch=[place, starts],
        tokens=tokens,
    )


def attend_back_kernel(
    place,
    starts,
    q_ref,
    k_ref,
    v_ref,
    grad_ref,
    out_ref,
    lse_ref,
    cosine,
    sine_up,
    sine_down,
    joined_ref,
    send_ref,
    sum_ref,
    query_grad,
    delta,
):
    block = pl.program_id(1)
    heads, blocks, rows = q_ref.shape[0], q_ref.shape[2], q_ref.shape[-2]
    here = place[0]
    documents = Documents(place, starts, pl.program_id(0), rows)
    high = documents.last_query_block(block, blocks)
    scaling = 1.0 / math.sqrt(HD)

    @pl.when(block == 0)
    def _():
        query_grad[...] = jnp.zeros_like(query_grad)

        def inner(j, carry):
            for head in range(heads):
                cols = slice(head * HD, (head + 1) * HD)
                product = grad_ref[0, j, :, cols].astype(F32) * out_ref[0, j, :, cols].astype(F32)
                delta[head, j] = jnp.sum(product.T, axis=0, keepdims=True)
            return carry

        lax.fori_loop(0, blocks, inner, 0)

    own = block ^ here
    key_places = block * rows + lax.broadcasted_iota(jnp.int32, (rows, 1), 0)

    def step(number, carry):
        at = number ^ here
        query_places = number * rows + lax.broadcasted_iota(jnp.int32, (1, rows), 1)
        allowed = (key_places >= documents.begin(query_places)) & (key_places <= query_places)
        results = []
        for head in range(heads):
            key_grad, value_grad = carry[head]
            key = k_ref[head, 0, own]
            value = v_ref[head, 0, own]
            query = q_ref[head, 0, at]
            grad = grad_ref[0, at, :, head * HD : (head + 1) * HD]
            scores = lax.dot_general(key, query, CONTRACT_LAST, preferred_element_type=F32)
            scores = scores * (scaling * LOG2E) - lse_ref[head, 0, at]
            weights = jnp.where(allowed, jnp.exp2(scores), 0.0)
            weight_grad = lax.dot_general(value, grad, CONTRACT_LAST, preferred_element_type=F32)
            score_grad = (weights * (weight_grad - delta[head, at]) * scaling).astype(BF16)
            value_grad = value_grad + jnp.dot(
                weights.astype(BF16), grad, preferred_element_type=F32
            )
            key_grad = key_grad + jnp.dot(score_grad, query, preferred_element_type=F32)
            query_grad[head, at] = query_grad[head, at] + lax.dot_general(
                score_grad, key, CONTRACT_FIRST, preferred_element_type=F32
            )
            results.append((key_grad, value_grad))
        return tuple(results)

    empty = jnp.zeros((rows, HD), F32)
    results = lax.fori_loop(block, high + 1, step, ((empty, empty),) * heads)
    tables = (cosine[0, own], -sine_up[0, own], -sine_down[0, own])
    for head, (key_grad, value_grad) in enumerate(results):
        at = head * 3 * HD
        joined_ref[0, own, :, at + HD : at + 2 * HD] = rope(key_grad, *tables).astype(BF16)
        joined_ref[0, own, :, at + 2 * HD : at + 3 * HD] = value_grad.astype(BF16)

    @pl.when(block == blocks - 1)
    def _():
        def inner(j, carry):
            tables = (cosine[0, j], -sine_up[0, j], -sine_down[0, j])
            for head in range(heads):
                at = head * 3 * HD
                joined_ref[0, j, :, at : at + HD] = rope(query_grad[head, j], *tables).astype(BF16)
            send_ref[j] = joined_ref[0, j]
            return carry + jnp.sum(joined_ref[0, j].astype(F32), axis=0, keepdims=True)

        sum_ref[0] = lax.fori_loop(0, blocks, inner, jnp.zeros((1, heads * 3 * HD), F32))


def attend_back(place, starts, queries, keys, values, grad, out, log_sums, tables, tokens):
    heads, seqs, blocks, rows, _ = queries.shape
    joined_cols = heads * 3 * HD
    head_spec = pl.BlockSpec((heads, 1, blocks, rows, HD), lambda s, i, *_: (0, s, 0, 0, 0))
    side = pl.BlockSpec((1, blocks, rows, heads * HD), lambda s, i, *_: (s, 0, 0, 0))
    table = pl.BlockSpec((1, blocks, rows, HD), lambda s, i, *_: (s, 0, 0, 0))
    pairs = heads * seqs * blocks * (blocks + 1) // 2
    return launch(
        attend_back_kernel,
        [queries, keys, values, grad, out, log_sums]
        + [item.reshape(seqs, blocks, rows, HD) for item in tables],
        [
            head_spec,
            head_spec,
            head_spec,
            side,
            side,
            pl.BlockSpec((heads, 1, blocks, 1, rows), lambda s, i, *_: (0, s, 0, 0, 0)),
            table,
            table,
            table,
        ],
        (seqs, blocks),
        [
            pl.BlockSpec((1, blocks, rows, joined_cols), lambda s, i, *_: (s, 0, 0, 0)),
            pl.BlockSpec((blocks, rows, joined_cols), lambda s, i, *_: (0, 0, 0)),
            pl.BlockSpec((1, 1, joined_cols), lambda s, i, *_: (s, 0, 0)),
        ],
        [
            jax.ShapeDtypeStruct((seqs, blocks, rows, joined_cols), BF16),
            jax.ShapeDtypeStruct((blocks, rows, joined_cols), BF16),
            jax.ShapeDtypeStruct((seqs, 1, joined_cols), F32),
        ],
        "attend_back",
        cost(pairs * 50 * rows * rows * HD, 12 * queries.size * 2),
        prefetch=[place, starts],
        tokens=tokens,
        scratch_shapes=[
            pltpu.VMEM((heads, blocks, rows, HD), F32),
            pltpu.VMEM((heads, blocks, 1, rows), F32),
        ],
    )


def expand_kernel(normed, weight, bias, activated, send, slope):
    pre = row_product(normed, weight, weight.shape[2]) + bias[...]
    share = 0.5 + 0.5 * lax.erf(pre * math.sqrt(0.5))
    density = jnp.exp2(pre * pre * (-0.5 * LOG2E)) * (1.0 / math.sqrt(2.0 * math.pi))
    result = (pre * share).astype(BF16)
    activated[...] = result
    send[...] = result
    slope[...] = (share + pre * density).astype(BF16)


def later_half(tile, width, steps):
    half = steps // 2
    return pl.BlockSpec((tile, width), lambda i: (jnp.maximum(i - half, 0), 0))


def expand(normed, weight, bias, tokens):
    rows, model_width = normed.shape
    cols = weight.shape[3]
    tile = 512
    steps = rows // tile
    out = pl.BlockSpec((tile, cols), lambda i: (i, 0))
    shape = jax.ShapeDtypeStruct((rows, cols), BF16)
    return launch(
        expand_kernel,
        [normed, weight, bias],
        [pl.BlockSpec((tile, model_width), lambda i: (i, 0)), whole_spec(weight), whole_spec(bias)],
        (steps,),
        [out, later_half(tile, cols, steps), out],
        [shape, jax.ShapeDtypeStruct((rows // 2, cols), BF16), shape],
        "expand",
        cost(
            2 * rows * model_width * cols,
            2 * (rows * model_width + weight.size + 2 * rows * cols),
        ),
        tokens=tokens,
    )


def by_columns(weight):
    groups = weight.shape[0] // 2
    return pl.BlockSpec(
        (2, 1) + weight.shape[2:], lambda i: (lax.rem(i, groups), lax.div(i, groups), 0, 0)
    )


def output_piece(j, pieces, attended, activated, dense, contract, sums, tokens):
    tile = attended[1].shape[0] // pieces
    groups, cores, _, share = dense[0].shape
    steps = groups * cores // 2
    lefts = [*attended, *activated]
    rights = [*dense, *contract]
    extras = sums.extras(j)

    def kernel(*refs):
        outs = refs[8 + len(extras) :]
        arrived = [(q, ref) for (q, _), ref in zip(extras, refs[8:])]
        for n in range(2):
            total = None
            for left, right in zip(refs[:4], refs[4:8]):
                part = jnp.dot(left[...], right[n, 0], preferred_element_type=F32)
                total = part if total is None else total + part
            finish_piece(total, n * share, arrived, outs)

    specs, shapes = piece_specs(tile, 2 * share, steps, sums.splits(j))
    result = launch(
        kernel,
        lefts + rights + [item for _, item in extras],
        [pl.BlockSpec((tile, item.shape[1]), lambda i: (j, 0)) for item in lefts]
        + [by_columns(item) for item in rights]
        + [pl.BlockSpec((tile // 2, 2 * share), lambda i: (0, i))] * len(extras),
        (steps,),
        specs,
        shapes,
        "output_piece",
        cost(4 * tile * sum(item.size for item in rights), 4 * sum(item.size for item in rights)),
        tokens=tokens,
    )
    sums.pieces[j] = result if sums.splits(j) else result[0]
    return result[0]


def dense_back_kernel(grad_ref, att_ref, dense, out, blocks, total):
    step = pl.program_id(0)
    share = dense.shape[3]

    @pl.when(step == 0)
    def _():
        total[...] = jnp.zeros_like(total)

    out[...] = column_back(grad_ref, dense, share).astype(BF16)
    total[...] += lax.dot_general(
        att_ref[...], grad_ref[...], CONTRACT_FIRST, preferred_element_type=F32
    )

    @pl.when(step == pl.num_programs(0) - 1)
    def _():
        for z, c, at in chunks_of(dense):
            blocks[z, c] = total[:, at * share : (at + 1) * share].T.astype(BF16)


def dense_back(grad, attended, dense, tokens):
    rows, width = grad.shape
    groups, cores, cols, share = dense.shape
    turned = jax.ShapeDtypeStruct((groups, cores, share, cols), BF16)
    tile = 512
    return launch(
        dense_back_kernel,
        [grad, attended, dense],
        [
            pl.BlockSpec((tile, width), lambda i: (i, 0)),
            pl.BlockSpec((tile, cols), lambda i: (i, 0)),
            whole_spec(dense),
        ],
        (rows // tile,),
        [pl.BlockSpec((tile, cols), lambda i: (i, 0)), whole_spec(turned)],
        [jax.ShapeDtypeStruct((rows, cols), BF16), turned],
        "dense_back",
        cost(4 * rows * dense.size, 2 * (rows * (width + cols) + dense.size)),
        tokens=tokens,
        scratch_shapes=[pltpu.VMEM((cols, width), F32)],
    )


def pre_grad_kernel(grad_ref, slope, contract, out, send, sums):
    @pl.when(pl.program_id(0) == 0)
    def _():
        sums[...] = jnp.zeros_like(sums)

    part = column_back(grad_ref, contract, contract.shape[3]) * slope[...].astype(F32)
    part = part.astype(BF16)
    out[...] = part
    send[...] = part
    sums[...] += jnp.sum(part.astype(F32), axis=0, keepdims=True)


def pre_grad_of(grad, slope, contract, tokens):
    rows, width = grad.shape
    cols = contract.shape[2]
    tile = 512
    steps = rows // tile
    return launch(
        pre_grad_kernel,
        [grad, slope, contract],
        [
            pl.BlockSpec((tile, width), lambda i: (i, 0)),
            pl.BlockSpec((tile, cols), lambda i: (i, 0)),
            whole_spec(contract),
        ],
        (steps,),
        [
            pl.BlockSpec((tile, cols), lambda i: (i, 0)),
            later_half(tile, cols, steps),
            pl.BlockSpec((1, cols), lambda i: (0, 0)),
        ],
        [
            jax.ShapeDtypeStruct((rows, cols), BF16),
            jax.ShapeDtypeStruct((rows // 2, cols), BF16),
            jax.ShapeDtypeStruct((1, cols), F32),
        ],
        "pre_grad",
        cost(2 * rows * contract.size, 2 * (rows * width + contract.size + 2 * rows * cols)),
        tokens=tokens,
    )


def normed_grad_piece(
    j, pieces, joined, pre, joined_weight, expand_weight, normal, gain1, gain2, sums, tokens
):
    tile = joined[1].shape[0] // pieces
    groups, cores, share, _ = joined_weight[0].shape
    steps = groups * cores // 2
    lefts = [*joined, *pre]
    rights = [*joined_weight, *expand_weight]
    extras = sums.extras(j)

    def kernel(*refs):
        normal, gain1, gain2 = refs[8:11]
        arrived = [(q, ref) for (q, _), ref in zip(extras, refs[11:])]
        *outs, along = refs[11 + len(extras) :]
        for n in range(2):

            def back(at):
                return lax.dot_general(
                    refs[at][...], refs[at + 4][n, 0], CONTRACT_LAST, preferred_element_type=F32
                )

            cols = slice(n * share, (n + 1) * share)
            first, second = back(0) + back(1), back(2) + back(3)
            rows = normal[:, cols].astype(F32)
            along[0:1, cols] = jnp.sum(first * rows, axis=0, keepdims=True)
            along[1:2, cols] = jnp.sum(first, axis=0, keepdims=True)
            along[2:3, cols] = jnp.sum(second * rows, axis=0, keepdims=True)
            along[3:4, cols] = jnp.sum(second, axis=0, keepdims=True)
            finish_piece(
                first * gain1[:, cols] + second * gain2[:, cols], n * share, arrived, outs
            )

    row = pl.BlockSpec((1, 2 * share), lambda i: (0, i))
    specs, shapes = piece_specs(tile, 2 * share, steps, sums.splits(j))
    *result, along = launch(
        kernel,
        lefts + rights + [normal, gain1, gain2] + [item for _, item in extras],
        [pl.BlockSpec((tile, item.shape[1]), lambda i: (j, 0)) for item in lefts]
        + [by_columns(item) for item in rights]
        + [pl.BlockSpec((tile, 2 * share), lambda i: (j, i)), row, row]
        + [pl.BlockSpec((tile // 2, 2 * share), lambda i: (0, i))] * len(extras),
        (steps,),
        specs + [pl.BlockSpec((8, 2 * share), lambda i: (0, i))],
        shapes + [jax.ShapeDtypeStruct((8, steps * 2 * share), F32)],
        "normed_grad_piece",
        cost(4 * tile * sum(item.size for item in rights), 4 * sum(item.size for item in rights)),
        tokens=tokens,
    )
    sums.pieces[j] = result if sums.splits(j) else result[0]
    return along


def rows_at(half, width, here):
    if here:
        return pl.BlockSpec((1, half, width), lambda i, place: (place[1], i, 0))
    return pl.BlockSpec((1, half, width), lambda i, place: (1 - place[1], i, 0))


def finish_tile(body, name, place, operands, whole, tile, width, tokens=()):
    half = tile // 2
    listed, specs, picks = [], [], []
    for pair in operands:
        if not isinstance(pair, list):
            picks.append((len(listed), False))
            listed.append(pair)
            specs.append(pl.BlockSpec((1, half, width), lambda i, place: (place[1], i, 0)))
        elif pair[0][0] is pair[1][0] and (pair[0][1], pair[1][1]) == (0, 1):
            picks.append((len(listed), False))
            listed.append(pair[0][0])
            specs.append(pl.BlockSpec((half, width), lambda i, place: (i, 0)))
        else:
            picks.append((len(listed), True))
            for item, at in pair:
                listed.append(item)
                specs.append(pl.BlockSpec((half, width), lambda i, place, at=at: (at, 0)))
    count = len(listed)

    def kernel(place, *refs):
        both, own = refs[count + len(whole) :]
        first = pl.program_id(0) == 0
        values = [
            jnp.where(first, refs[at][...], refs[at + 1][...])
            if pair
            else refs[at][...].reshape(half, width)
            for at, pair in picks
        ]
        result = body(values, refs[count : count + len(whole)]).astype(BF16)
        both[0] = result
        own[...] = result

    return launch(
        kernel,
        listed + list(whole),
        specs + [pl.BlockSpec(item.shape, lambda i, place: (0, 0)) for item in whole],
        (2,),
        [rows_at(half, width, True), pl.BlockSpec((half, width), lambda i, place: (i, 0))],
        [
            jax.ShapeDtypeStruct((2, tile, width), BF16),
            jax.ShapeDtypeStruct((tile, width), BF16),
        ],
        name,
        cost(20 * tile * width, 20 * tile * width),
        prefetch=[place],
        tokens=tokens,
    )


def pick_other(place, total, tokens):
    _, rows, cols = total.shape

    def pick(place, value, out):
        out[...] = value[0]

    other = launch(
        pick,
        [total],
        [pl.BlockSpec((1, rows, cols), lambda i, place: (1 - place[1], 0, 0))],
        (1,),
        pl.BlockSpec((rows, cols), lambda i, place: (0, 0)),
        jax.ShapeDtypeStruct((rows, cols), BF16),
        "pick_other",
        cost(1, 4 * rows * cols),
        prefetch=[place],
        tokens=tokens,
    )
    return swap(other, "branch", 1)


def join_cores(place, total, other, straight, tokens):
    _, rows, cols = total.shape
    turned = cols - straight

    def join(place, mine, others, *outs):
        value = jnp.where(pl.program_id(0) == 0, mine[0], others[...]).astype(F32)
        if straight:
            outs[0][...] = value[:, :straight]
        if turned:
            outs[-1][...] = value[:, straight:].T

    specs, shapes = [], []
    if straight:
        specs.append(pl.BlockSpec((rows, straight), lambda i, place: (0, place[1] ^ i)))
        shapes.append(jax.ShapeDtypeStruct((rows, 2 * straight), F32))
    if turned:
        specs.append(pl.BlockSpec((turned, rows), lambda i, place: (place[1] ^ i, 0)))
        shapes.append(jax.ShapeDtypeStruct((2 * turned, rows), F32))
    return launch(
        join,
        [total, other],
        [
            pl.BlockSpec((1, rows, cols), lambda i, place: (place[1], 0, 0)),
            pl.BlockSpec((rows, cols), lambda i, place: (0, 0)),
        ],
        (2,),
        specs,
        shapes,
        "finish_weight",
        cost(1, 16 * rows * cols),
        prefetch=[place],
        tokens=tokens,
    )


def fill_other(place, both, other, tokens=()):
    tile, width = other.shape

    def kernel(place, value, out):
        out[0] = value[...]

    return launch(
        kernel,
        [other],
        [pl.BlockSpec((tile // 2, width), lambda i, place: (i, 0))],
        (2,),
        rows_at(tile // 2, width, False),
        jax.ShapeDtypeStruct(both.shape, BF16),
        "fill_other",
        cost(1, 4 * tile * width),
        prefetch=[place],
        tokens=tokens,
        held=[both],
    )


def per_device(
    block_input,
    first_norm_gain,
    first_norm_bias,
    second_norm_gain,
    second_norm_bias,
    query_key_value,
    query_key_value_bias,
    attention_dense,
    attention_dense_bias,
    expand_weight,
    expand_bias,
    contract_weight,
    contract_bias,
    document_starts,
    output_grad,
):
    seqs, tile, model_width = block_input.shape
    tiles = lax.axis_size("tp")
    groups = lax.axis_size("seq")
    core = lax.axis_index("branch")
    here = lax.axis_index("tp")
    first_core = core == 0
    length = tile * tiles
    rows_in_all = length * seqs
    share = query_key_value.shape[0]

    def by_core(mine, others):
        return jnp.where(first_core, mine, others), jnp.where(first_core, others, mine)

    def halves_of(value, axis):
        size = value.shape[axis] // 2
        return (
            lax.dynamic_slice_in_dim(value, core * size, size, axis),
            lax.dynamic_slice_in_dim(value, (1 - core) * size, size, axis),
        )

    place = jnp.stack([here, core]).astype(jnp.int32)

    input_halves = own_halves(place, block_input)
    near = {**gather_near(input_halves, 0), **gather_near(input_halves, 1)}

    def core_halves(weight, axis):
        mine, others = halves_of(weight, axis)
        return jnp.stack(by_core(mine, swap(others, "branch", 1)))

    def gather_seq(piece):
        return lax.all_gather(piece, "seq", axis=0)

    weight_pieces = [
        core_halves(query_key_value, 1),
        core_halves(expand_weight, 1),
        core_halves(attention_dense, 0),
        core_halves(contract_weight, 0),
    ]
    joined_weight, expand_full, dense_full, contract_full = map(gather_seq, weight_pieces)
    joined_bias = halves_of(query_key_value_bias, 0)[0].astype(F32)[None]
    hidden_bias = halves_of(expand_bias, 0)[0].astype(F32)[None]

    gain1 = first_norm_gain.astype(F32)[None]
    gain2 = second_norm_gain.astype(F32)[None]
    gains = (
        gain1,
        first_norm_bias.astype(F32)[None],
        gain2,
        second_norm_bias.astype(F32)[None],
    )
    tables = rotary_tables(place, document_starts, rows_in_all, weight_pieces)
    grad_halves = own_halves(place, output_grad, [tables[0]])
    grad_rows = place_piece(0, place, output_grad, rows_in_all, (), grad_halves)
    *normed, mark = norm_piece(
        0, place, block_input, rows_in_all, gains, (), [tables[0], grad_rows]
    )
    near = in_pieces(hold_all(near, mark), {})
    far = gather_far(near)
    for j in sorted(near):
        *normed, mark = norm_piece(
            j, place, with_other_core(near[j]), rows_in_all, gains, normed, []
        )
    heads_held = ()
    far_from = tiles
    if tiles == 4:
        heads_held = project(0, 3, normed[1], joined_weight, joined_bias, tables, ())
        far_from = 3
    for j in sorted(far):
        last_items = [hold(item, mark) for item in far[j]]
        *normed, mark = norm_piece(
            j, place, with_other_core(last_items), rows_in_all, gains, normed, heads_held[:1]
        )
    heads_held = project(
        far_from % tiles, tiles, normed[1], joined_weight, joined_bias, tables, heads_held
    )
    normal, first_normed, second_normed = normed
    queries, keys, values = heads_held

    first = gather_near([hold(item, *last_items) for item in grad_halves], 0)
    first = hold_all(first, queries)
    second = gather_near([hold(item, *first.values()) for item in grad_halves], 1)
    attended, attended_send, log_sums = attend(
        place, document_starts, queries, keys, values, [*first.values()]
    )
    attended_flat = attended.reshape(rows_in_all, -1)
    near = in_pieces(first, hold_all(second, log_sums))
    far = gather_far(near)
    activated, activated_send, slope = expand(
        second_normed, expand_full, hidden_bias, [item for j in near for item in near[j]]
    )
    near = {
        j: items + [hold(swap(item, "branch", 1), slope) for item in items]
        for j, items in near.items()
    }
    far = {j: [hold(item, slope) for item in items] for j, items in far.items()}
    arrived = [item for items in [*near.values(), *far.values()] for item in items]
    far = {j: with_other_core(items) for j, items in far.items()}
    for j, items in {**near, **far}.items():
        grad_rows = place_piece(j, place, items, rows_in_all, [grad_rows], [slope])

    def weight_grad(left, right):
        return lax.dot_general(left, right, CONTRACT_FIRST, preferred_element_type=F32).astype(BF16)

    def in_order(part):
        return part.reshape(2, groups, share, part.shape[1]).transpose(1, 0, 2, 3)

    def scatter(blocks):
        return lax.psum_scatter(blocks, "seq", scatter_dimension=0, tiled=False)

    def exchanged(own, send, *tokens):
        send = send.reshape(-1, send.shape[-1])
        return own.reshape(-1, own.shape[-1]), swap(hold(send, *tokens) if tokens else send, "branch", 1)

    def with_other_weight(weight):
        return weight, swap(weight, "branch", 1)

    attended_pair = exchanged(attended, attended_send, *arrived)
    activated_pair = exchanged(activated, activated_send, *arrived)
    contract_blocks = in_order(weight_grad(grad_rows, activated))
    contract_total = scatter(contract_blocks)
    contract_full = hold(contract_full, contract_blocks)
    pre_grad, pre_send, pre_sums = pre_grad_of(
        grad_rows, slope, contract_full, [contract_blocks]
    )
    pre_pair = exchanged(pre_grad, pre_send)
    contract_pair = with_other_weight(contract_full)
    expand_blocks = in_order(weight_grad(second_normed, pre_grad))
    expand_total = scatter(expand_blocks)
    dense_pair = with_other_weight(dense_full)
    order = sorted(range(1, tiles), key=lambda j: (-bin(j).count("1"), j))
    outputs = TileSum()

    def output(j, *tokens):
        return output_piece(
            j, tiles, attended_pair, activated_pair, dense_pair, contract_pair, outputs, tokens
        )

    mark = expand_blocks
    operands = []
    for number, j in enumerate(order):
        if number and bin(order[number - 1]).count("1") > bin(j).count("1"):
            if not outputs.pieces.get(0) is None:
                operands += outputs.land(mark)
            else:
                attended_grad, dense_blocks = dense_back(
                    grad_rows, attended_flat, dense_full, [mark, *operands]
                )
                mark = output(0, attended_grad)
                operands = outputs.land(mark)
        mark = output(j, mark, *operands)
        operands = outputs.send() if outputs.complete(j) else []
    operands += outputs.send()
    landed = []
    joined_grad, joined_send, joined_sums = attend_back(
        place,
        document_starts,
        queries,
        keys,
        values,
        attended_grad.reshape(attended.shape),
        attended,
        log_sums,
        tables,
        [mark, *operands],
    )
    landed = outputs.land(joined_sums)
    joined_pair = exchanged(joined_grad, joined_send, *landed)
    joined_weight_pair = with_other_weight(joined_weight)
    expand_weight_pair = with_other_weight(expand_full)
    joined_grad = joined_pair[0]
    inputs = TileSum()
    sums = jnp.zeros((8, model_width), F32)
    mark = joined_sums
    wait = landed
    joined_blocks = None
    for number, j in enumerate(order + [0]):
        if number and j and bin(order[number - 1]).count("1") > bin(j).count("1"):
            if joined_blocks is None:
                part = weight_grad(hold(first_normed, mark, *wait), joined_grad)
                wait = inputs.land(part)
                joined_blocks = jnp.concatenate(
                    [in_order(hold(part, *wait)), dense_blocks], axis=3
                )
                joined_total = scatter(joined_blocks)
                mark = joined_blocks
            else:
                wait = inputs.land(mark)
        part = normed_grad_piece(
            j,
            tiles,
            joined_pair,
            pre_pair,
            joined_weight_pair,
            expand_weight_pair,
            normal,
            gain1,
            gain2,
            inputs,
            [mark, *wait],
        )
        sums = sums + part
        mark = part
        wait = inputs.send()
    landed = inputs.land(mark)

    biases = (
        attention_dense_bias.astype(F32)[None],
        contract_bias.astype(F32)[None],
    )

    def output_body(values, whole):
        return add_up(values) + whole[0][...] + whole[1][...]

    def all_sum_beside(value, axis, others):
        size = lax.axis_size(axis)
        bit = 1
        while bit < size:
            arrived = swap(value, axis, bit)
            if others:
                arrived = hold(arrived, *others.pop(0)())
            value = value + arrived
            bit *= 2
        return value

    kept = {}

    def first_beside():
        kept["both"], kept["own"] = finish_tile(
            output_body,
            "finish_output",
            place,
            [block_input] + outputs.terms(),
            biases,
            tile,
            model_width,
            [mark],
        )
        return [kept["own"]]

    def second_beside():
        kept["contract"] = pick_other(place, contract_total, [kept["own"]])
        kept["expand"] = pick_other(place, expand_total, [kept["contract"]])
        return [kept["expand"]]

    def third_beside():
        (kept["contract_grad"],) = join_cores(
            place, contract_total, kept["contract"], 0, [kept["expand"]]
        )
        return [kept["contract_grad"], *landed]

    def fourth_beside():
        (kept["expand_grad"],) = join_cores(
            place,
            expand_total,
            kept["expand"],
            expand_total.shape[2],
            [kept["contract_grad"]],
        )
        return [kept["expand_grad"]]

    def fifth_beside():
        kept["output"] = fill_other(
            place, kept["both"], swap(kept["own"], "branch", 1), [kept["expand_grad"]]
        )
        return [kept["output"]]

    others = [first_beside, second_beside, third_beside, fourth_beside, fifth_beside]
    joined_bias_part = jnp.sum(joined_sums, axis=0).reshape(-1)
    hidden_bias_part = pre_sums[0]
    grad_own = lax.dynamic_index_in_dim(output_grad, core, 0, False)
    small = jnp.concatenate(
        [
            sums[:4].reshape(-1),
            jnp.sum(grad_own.astype(F32), axis=0),
            joined_bias_part,
            hidden_bias_part,
        ]
    )
    everywhere = 5 * model_width
    small = all_sum_beside(hold(small, mark), "seq", others)
    per_core = small[everywhere:]
    both = jnp.stack(by_core(per_core, swap(per_core, "branch", 1)))
    query_key_value_bias_grad = both[:, : joined_bias_part.shape[0]].reshape(-1)
    expand_bias_grad = both[:, joined_bias_part.shape[0] :].reshape(-1)
    shared = all_sum_beside(small[:everywhere], "tp", others)
    shared = all_sum_beside(shared, "branch", others).reshape(5, model_width)
    while others:
        others.pop(0)()
    block_output, contract_grad = kept["output"], kept["contract_grad"]
    expand_grad = kept["expand_grad"]
    joined_other = pick_other(place, joined_total, [shared, block_output])

    def input_body(values, whole):
        x, grad = values[0].astype(F32), values[1].astype(F32)
        total = add_up(values[2:])
        centred = x - jnp.mean(x, axis=-1, keepdims=True)
        rate = lax.rsqrt(jnp.mean(centred * centred, axis=-1, keepdims=True) + EPSILON)
        n = centred * rate
        middle = jnp.mean(total, axis=-1, keepdims=True)
        along = jnp.mean(total * n, axis=-1, keepdims=True)
        return grad + rate * (total - middle - n * along)

    input_both, input_grad_own = finish_tile(
        input_body,
        "finish_input",
        place,
        [block_input, output_grad] + inputs.terms(),
        (),
        tile,
        model_width,
        [joined_other],
    )
    query_key_value_grad, dense_grad = join_cores(
        place, joined_total, joined_other, joined_weight.shape[3], [input_grad_own]
    )
    input_grad = fill_other(
        place, input_both, swap(input_grad_own, "branch", 1), [query_key_value_grad]
    )
    return (
        block_output,
        input_grad,
        shared[0],
        shared[1],
        shared[2],
        shared[3],
        query_key_value_grad,
        query_key_value_bias_grad,
        dense_grad,
        shared[4],
        expand_grad,
        expand_bias_grad,
        contract_grad,
        shared[4],
    )


def solution(mesh):
    in_specs = (
        P("seq", "tp", None),
        P(),
        P(),
        P(),
        P(),
        P(("branch", "seq"), "tp"),
        P("tp"),
        P("tp", ("branch", "seq")),
        P(),
        P(("branch", "seq"), "tp"),
        P("tp"),
        P("tp", ("branch", "seq")),
        P(),
        P("seq", None),
        P("seq", "tp", None),
    )
    out_specs = (
        P("seq", "tp", None),
        P("seq", "tp", None),
        P(),
        P(),
        P(),
        P(),
        P(("branch", "seq"), "tp"),
        P("tp"),
        P("tp", ("branch", "seq")),
        P(),
        P(("branch", "seq"), "tp"),
        P("tp"),
        P("tp", ("branch", "seq")),
        P(),
    )
    return jax.shard_map(
        per_device, mesh=mesh, in_specs=in_specs, out_specs=out_specs, check_vma=False
    )
```

profile of v0, /device:TPU:0, one launch (start us, length us, event | category | flops | bytes accessed | tf_op | source)
XLA Modules:
  0.0 622.6 jit_solution(15357614125008739156)
XLA Ops:
  31.4 10.8 %rotary_tables.1 = (f32[4096,128]{1,0:T(8,128)}, f32[4096,128]{1,0:T(8,128)}, f32[4096,128]{1,0:T(8,128)}) custom-call(s32[2]{0:T(128)} %pad_add_fusion.refs_0_, s32[2,8]{1,0:T(2,128)} %refs_1_.15, bf16[2,256,768]{2,1,0:T(8,128)(2,1)} %pad_maximum_fusion.3.refs_2_, bf16[2,256,1024]{2,1,0:T(8,128)(2,1)} %pad_maximum_fusion.1.refs_3_, ...), custom_call_target="tpu_custom_call" | custom-call | flops 1048577 | bytes 503317 | tf_op jit(solution)/shard_map/rotary_tables/pallas_call | solution.py:54
  45.8 5.4 place_piece.4.refs_10_.refs_5_
  51.2 9.7 %norm_piece.4 = (bf16[4096,2048]{1,0:T(8,128)(2,1)}, bf16[4096,2048]{1,0:T(8,128)(2,1)}, bf16[4096,2048]{1,0:T(8,128)(2,1)}, f32[8,128]{1,0:T(8,128)}) custom-call(s32[2]{0:T(128)} %pad_add_fusion.refs_0_, bf16[2,512,2048]{2,1,0:T(8,128)(2,1)} %refs_1_.17, bf16[2,512,2048]{2,1,0:T(8,128)(2,1)} %refs_1_.17, bf16[2,512,2048]{2,1,0:T(8,128)(2,1)} %refs_1_.17, ...), custom_call_target="tpu_custom_call" | custom-call | flops 671089 | bytes 671089 | tf_op jit(solution)/shard_map/norm_piece/pallas_call | solution.py:54
  61.9 8.0 %collective-permute-done.refs_0_ = bf16[256,2048]{1,0:T(8,128)(2,1)} collective-permute-done((bf16[256,2048]{1,0:T(8,128)(2,1)}, bf16[256,2048]{1,0:T(8,128)(2,1)}, u32[]{:S(2)}, u32[]{:S(2)}) %collective-permute-start) | collective-permute-done | bytes 1048608 | tf_op jit(solution)/shard_map/ppermute | solution.py:93
  78.4 9.5 %norm_piece.5 = (bf16[4096,2048]{1,0:T(8,128)(2,1)}, bf16[4096,2048]{1,0:T(8,128)(2,1)}, bf16[4096,2048]{1,0:T(8,128)(2,1)}, f32[8,128]{1,0:T(8,128)}) custom-call(s32[2]{0:T(128)} %pad_add_fusion.refs_0_, bf16[256,2048]{1,0:T(8,128)(2,1)} %hold.40.refs_1_, ...), custom_call_target="tpu_custom_call", output_to_operand_aliasing={{0}: (9, {}), {1}: (10, {}), {2}: (11, {})} | custom-call | flops 671089 | bytes 671089 | tf_op jit(solution)/shard_map/norm_piece/pallas_call | solution.py:54
  89.2 9.6 %norm_piece.6 = (bf16[4096,2048]{1,0:T(8,128)(2,1)}, bf16[4096,2048]{1,0:T(8,128)(2,1)}, bf16[4096,2048]{1,0:T(8,128)(2,1)}, f32[8,128]{1,0:T(8,128)}) custom-call(s32[2]{0:T(128)} %pad_add_fusion.refs_0_, bf16[256,2048]{1,0:T(8,128)(2,1)} %hold.41.refs_1_, ...), custom_call_target="tpu_custom_call", output_to_operand_aliasing={{0}: (9, {}), {1}: (10, {}), {2}: (11, {})} | custom-call | flops 671089 | bytes 671089 | tf_op jit(solution)/shard_map/norm_piece/pallas_call | solution.py:54
  108.3 17.0 %project.2 = (bf16[2,2,4,512,128]{4,3,2,1,0:T(8,128)(2,1)}, bf16[2,2,4,512,128]{4,3,2,1,0:T(8,128)(2,1)}, bf16[2,2,4,512,128]{4,3,2,1,0:T(8,128)(2,1)}) custom-call(bf16[4096,2048]{1,0:T(8,128)(2,1)} %get-tuple-element.86.refs_0_.refs_10_, bf16[4,2,256,768]{3,2,1,0:T(8,128)(2,1)} %bitcast.68, f32[1,768]{1,0:T(1,128)} %reshape.107.refs_2_, ...), custom_call_target="tpu_custom_call" | custom-call | flops 193273536 | bytes 408945 | tf_op jit(solution)/shard_map/project/pallas_call | solution.py:54
  126.3 9.7 %norm_piece.7 = (bf16[4096,2048]{1,0:T(8,128)(2,1)}, bf16[4096,2048]{1,0:T(8,128)(2,1)}, bf16[4096,2048]{1,0:T(8,128)(2,1)}, f32[8,128]{1,0:T(8,128)}) custom-call(s32[2]{0:T(128)} %pad_add_fusion.refs_0_, bf16[256,2048]{1,0:T(8,128)(2,1)} %hold.44.refs_1_, ...), custom_call_target="tpu_custom_call", output_to_operand_aliasing={{0}: (9, {}), {1}: (10, {}), {2}: (11, {})} | custom-call | flops 671089 | bytes 671089 | tf_op jit(solution)/shard_map/norm_piece/pallas_call | solution.py:54
  136.0 8.5 %project.3 = (bf16[2,2,4,512,128]{4,3,2,1,0:T(8,128)(2,1)}, bf16[2,2,4,512,128]{4,3,2,1,0:T(8,128)(2,1)}, bf16[2,2,4,512,128]{4,3,2,1,0:T(8,128)(2,1)}) custom-call(bf16[4096,2048]{1,0:T(8,128)(2,1)} %get-tuple-element.91.refs_0_, bf16[4,2,256,768]{3,2,1,0:T(8,128)(2,1)} %bitcast.69, ...), custom_call_target="tpu_custom_call", output_to_operand_aliasing={{0}: (6, {}), {1}: (7, {}), {2}: (8, {})} | custom-call | flops 64424512 | bytes 178258 | tf_op jit(solution)/shard_map/project/pallas_call | solution.py:54
  150.2 33.2 %attend.1 = (bf16[2,4,512,256]{3,2,1,0:T(8,128)(2,1)}, bf16[4,512,256]{2,1,0:T(8,128)(2,1)}, f32[2,2,4,1,512]{4,3,2,1,0:T(1,128)}) custom-call(s32[2]{0:T(128)} %pad_add_fusion.refs_0_, s32[2,8]{1,0:T(2,128)} %refs_1_.15, bf16[2,2,4,512,128]{4,3,2,1,0:T(8,128)(2,1)} %get-tuple-element.94.refs_1_.refs_2_, ...), custom_call_target="tpu_custom_call" | custom-call | flops 805306368 | bytes 167773 | tf_op jit(solution)/shard_map/attend/pallas_call | solution.py:54
  185.4 28.5 %expand.1 = (bf16[4096,1024]{1,0:T(8,128)(2,1)}, bf16[2048,1024]{1,0:T(8,128)(2,1)}, bf16[4096,1024]{1,0:T(8,128)(2,1)}) custom-call(bf16[4096,2048]{1,0:T(8,128)(2,1)} %get-tuple-element.100.refs_0_, bf16[4,2,256,1024]{3,2,1,0:T(8,128)(2,1)} %bitcast.75, f32[1,1024]{1,0:T(1,128)} %bitcast.147, bf16[256,2048]{1,0:T(8,128)(2,1)} %hold.47.refs_5_.refs_1_.refs_3_, ...), custom_call_target="tpu_custom_call" | custom-call | flops 343597376 | bytes 754975 | tf_op jit(solution)/shard_map/expand/pallas_call | solution.py:54
  216.0 5.4 place_piece.5.refs_5_
  228.8 5.4 place_piece.7.refs_0_
  234.2 22.7 %convolution_convert_fusion.1 = bf16[2048,1024]{1,0:T(8,128)(2,1)S(1)} fusion(bf16[4096,2048]{1,0:T(8,128)(2,1)} %place_piece.7.refs_0_, bf16[4096,1024]{1,0:T(8,128)(2,1)} %get-tuple-element.102.refs_2_), kind=kOutput, calls=%fused_computation.5 | convolution fusion | flops 17181966336 | bytes 29360128 | tf_op jit(solution)/shard_map/dot_general | solution.py:1176
  260.0 9.6 %all-gather.13.cloned.1.call-done = bf16[8,256,256]{2,1,0:T(8,128)(2,1)} async-done(((bf16[2,256,256]{2,1,0:T(8,128)(2,1)}), bf16[8,256,256]{2,1,0:T(8,128)(2,1)}) %all-gather.13.cloned.1.call-update) | async-done | bytes 1048592 | tf_op jit(solution)/shard_map/all_gather | solution.py:1105
  270.1 25.0 %pre_grad.1 = (bf16[4096,1024]{1,0:T(8,128)(2,1)}, bf16[2048,1024]{1,0:T(8,128)(2,1)}, f32[1,1024]{1,0:T(1,128)}) custom-call(bf16[4096,2048]{1,0:T(8,128)(2,1)} %place_piece.7.refs_0_, bf16[4096,1024]{1,0:T(8,128)(2,1)} %get-tuple-element.101.refs_1_.refs_6_, bf16[4,2,1024,256]{3,2,1,0:T(8,128)(2,1)} %hold.62.refs_2_.refs_6_, bf16[4,2,256,1024]{3,2,1,0:T(8,128)(2,1)} %bitcast.95), custom_call_target="tpu_custom_call" | custom-call | flops 343597376 | bytes 754975 | tf_op jit(solution)/shard_map/pre_grad/pallas_call | solution.py:54
  295.2 22.8 %convolution_convert_fusion = bf16[2048,1024]{1,0:T(8,128)(2,1)S(1)} fusion(bf16[4096,2048]{1,0:T(8,128)(2,1)} %get-tuple-element.100.refs_0_, bf16[4096,1024]{1,0:T(8,128)(2,1)} %get-tuple-element.104.refs_2_), kind=kOutput, calls=%fused_computation.4 | convolution fusion | flops 17181966336 | bytes 29360128 | tf_op jit(solution)/shard_map/dot_general | solution.py:1176
  321.8 9.9 %output_piece.4 = (bf16[256,2048]{1,0:T(8,128)(2,1)}, bf16[256,2048]{1,0:T(8,128)(2,1)}) custom-call(bf16[4096,256]{1,0:T(8,128)(2,1)} %bitcast.88, bf16[2048,256]{1,0:T(8,128)(2,1)} %copy-done.13, bf16[4096,1024]{1,0:T(8,128)(2,1)} %get-tuple-element.102.refs_2_, bf16[2048,1024]{1,0:T(8,128)(2,1)} %collective-permute-done.27.refs_3_, ...), custom_call_target="tpu_custom_call" | custom-call | flops 214748368 | bytes 419431 | tf_op jit(solution)/shard_map/output_piece/pallas_call | solution.py:54
  334.5 15.3 %dense_back.1 = (bf16[4096,256]{1,0:T(8,128)(2,1)}, bf16[4,2,256,256]{3,2,1,0:T(8,128)(2,1)}) custom-call(bf16[4096,2048]{1,0:T(8,128)(2,1)} %place_piece.7.refs_0_, bf16[4096,256]{1,0:T(8,128)(2,1)} %bitcast.89, bf16[4,2,256,256]{3,2,1,0:T(8,128)(2,1)} %bitcast.102, bf16[256,2048]{1,0:T(8,128)(2,1)} %get-tuple-element.105.refs_3_.refs_4_, ...), custom_call_target="tpu_custom_call" | custom-call | flops 171798688 | bytes 398459 | tf_op jit(solution)/shard_map/dense_back/pallas_call | solution.py:54
  349.8 10.0 %output_piece.5.refs_1_.refs_9_.refs_2_ = bf16[512,2048]{1,0:T(8,128)(2,1)} custom-call(bf16[4096,256]{1,0:T(8,128)(2,1)} %bitcast.90, bf16[2048,256]{1,0:T(8,128)(2,1)} %copy-done.13, bf16[4096,1024]{1,0:T(8,128)(2,1)} %get-tuple-element.102.refs_2_, bf16[2048,1024]{1,0:T(8,128)(2,1)} %collective-permute-done.27.refs_3_, ...), custom_call_target="tpu_custom_call" | custom-call | flops 214748368 | bytes 419431 | tf_op jit(solution)/shard_map/output_piece/pallas_call | solution.py:54
  361.9 10.1 %output_piece.6.refs_9_.refs_10_ = bf16[512,2048]{1,0:T(8,128)(2,1)} custom-call(bf16[4096,256]{1,0:T(8,128)(2,1)} %bitcast.91, bf16[2048,256]{1,0:T(8,128)(2,1)} %copy-done.13, bf16[4096,1024]{1,0:T(8,128)(2,1)} %get-tuple-element.102.refs_2_, bf16[2048,1024]{1,0:T(8,128)(2,1)} %collective-permute-done.27.refs_3_, bf16[4,2,256,256]{3,2,1,0:T(8,128)(2,1)} %bitcast.104, ...), custom_call_target="tpu_custom_call" | custom-call | flops 214748368 | bytes 419431 | tf_op jit(solution)/shard_map/output_piece/pallas_call | solution.py:54
  372.0 10.1 %output_piece.7.refs_11_.refs_12_ = bf16[512,2048]{1,0:T(8,128)(2,1)} custom-call(bf16[4096,256]{1,0:T(8,128)(2,1)} %bitcast.92, bf16[2048,256]{1,0:T(8,128)(2,1)} %copy-done.13, bf16[4096,1024]{1,0:T(8,128)(2,1)} %get-tuple-element.102.refs_2_, bf16[2048,1024]{1,0:T(8,128)(2,1)} %collective-permute-done.27.refs_3_, bf16[4,2,256,256]{3,2,1,0:T(8,128)(2,1)} %bitcast.105, ...), custom_call_target="tpu_custom_call" | custom-call | flops 214748368 | bytes 419431 | tf_op jit(solution)/shard_map/output_piece/pallas_call | solution.py:54
  384.1 54.0 %attend_back.1 = (bf16[2,4,512,768]{3,2,1,0:T(8,128)(2,1)}, bf16[4,512,768]{2,1,0:T(8,128)(2,1)}, f32[2,1,768]{2,1,0:T(1,128)}) custom-call(s32[2]{0:T(128)} %pad_add_fusion.refs_0_, s32[2,8]{1,0:T(2,128)} %refs_1_.15, bf16[2,2,4,512,128]{4,3,2,1,0:T(8,128)(2,1)} %get-tuple-element.94.refs_1_.refs_2_, ...), custom_call_target="tpu_custom_call" | custom-call | flops 1342177280 | bytes 503317 | tf_op jit(solution)/shard_map/attend_back/pallas_call | solution.py:54
  438.7 5.6 collective-permute-done.36.refs_1_
  444.3 13.1 %normed_grad_piece.4 = (bf16[256,2048]{1,0:T(8,128)(2,1)}, bf16[256,2048]{1,0:T(8,128)(2,1)}, f32[8,2048]{1,0:T(8,128)}) custom-call(bf16[4096,768]{1,0:T(8,128)(2,1)} %bitcast.81, bf16[2048,768]{1,0:T(8,128)(2,1)} %collective-permute-done.36.refs_1_, bf16[4096,1024]{1,0:T(8,128)(2,1)} %get-tuple-element.104.refs_2_, ...), custom_call_target="tpu_custom_call" | custom-call | flops 300647712 | bytes 587203 | tf_op jit(solution)/shard_map/normed_grad_piece/pallas_call | solution.py:54
  460.2 18.3 %convolution_convert_fusion.2.refs_1_.refs_0_ = bf16[2048,768]{1,0:T(8,128)(2,1)} fusion(bf16[4096,2048]{1,0:T(8,128)(2,1)} %hold.68, bf16[4096,768]{1,0:T(8,128)(2,1)S(1)} %bitcast.87), kind=kOutput, calls=%fused_computation.6 | convolution fusion | flops 12886474752 | bytes 26214400 | tf_op jit(solution)/shard_map/dot_general | solution.py:1176
  489.1 13.4 %normed_grad_piece.5 = (bf16[512,2048]{1,0:T(8,128)(2,1)}, f32[8,2048]{1,0:T(8,128)}) custom-call(bf16[4096,768]{1,0:T(8,128)(2,1)} %bitcast.82, bf16[2048,768]{1,0:T(8,128)(2,1)} %collective-permute-done.36.refs_1_, bf16[4096,1024]{1,0:T(8,128)(2,1)} %get-tuple-element.104.refs_2_, bf16[2048,1024]{1,0:T(8,128)(2,1)} %collective-permute-done.37.refs_3_, ...), custom_call_target="tpu_custom_call" | custom-call | flops 300647712 | bytes 587203 | tf_op jit(solution)/shard_map/normed_grad_piece/pallas_call | solution.py:54
  502.6 13.5 %normed_grad_piece.6 = (bf16[512,2048]{1,0:T(8,128)(2,1)}, f32[8,2048]{1,0:T(8,128)}) custom-call(bf16[4096,768]{1,0:T(8,128)(2,1)} %bitcast.83, bf16[2048,768]{1,0:T(8,128)(2,1)} %collective-permute-done.36.refs_1_, bf16[4096,1024]{1,0:T(8,128)(2,1)} %get-tuple-element.104.refs_2_, bf16[2048,1024]{1,0:T(8,128)(2,1)} %collective-permute-done.37.refs_3_, ...), custom_call_target="tpu_custom_call" | custom-call | flops 300647712 | bytes 587203 | tf_op jit(solution)/shard_map/normed_grad_piece/pallas_call | solution.py:54
  520.1 13.5 %normed_grad_piece.7 = (bf16[512,2048]{1,0:T(8,128)(2,1)}, f32[8,2048]{1,0:T(8,128)}) custom-call(bf16[4096,768]{1,0:T(8,128)(2,1)} %bitcast.84, bf16[2048,768]{1,0:T(8,128)(2,1)} %collective-permute-done.36.refs_1_, bf16[4096,1024]{1,0:T(8,128)(2,1)} %get-tuple-element.104.refs_2_, bf16[2048,1024]{1,0:T(8,128)(2,1)} %collective-permute-done.37.refs_3_, ...), custom_call_target="tpu_custom_call" | custom-call | flops 300647712 | bytes 587203 | tf_op jit(solution)/shard_map/normed_grad_piece/pallas_call | solution.py:54
  533.6 6.2 finish_output.1
  558.4 8.0 %collective-permute-done.48.refs_0_ = f32[12032]{0:T(1024)S(1)} collective-permute-done((f32[12032]{0:T(1024)S(1)}, f32[12032]{0:T(1024)S(1)}, u32[]{:S(2)}, u32[]{:S(2)}) %collective-permute-start.48) | collective-permute-done | bytes 48160 | tf_op jit(solution)/shard_map/ppermute | solution.py:93
  592.7 8.0 %finish_input.1 = (bf16[2,512,2048]{2,1,0:T(8,128)(2,1)}, bf16[512,2048]{1,0:T(8,128)(2,1)}) custom-call(s32[2]{0:T(128)} %pad_add_fusion.refs_0_, bf16[2,512,2048]{2,1,0:T(8,128)(2,1)} %refs_1_.17, bf16[2,512,2048]{2,1,0:T(8,128)(2,1)} %refs_2_.9, bf16[512,2048]{1,0:T(8,128)(2,1)} %get-tuple-element.124.refs_3_, bf16[512,2048]{1,0:T(8,128)(2,1)} %hold.72.refs_2_.refs_4_, ...), custom_call_target="tpu_custom_call" | custom-call | flops 419431 | bytes 419431 | tf_op jit(solution)/shard_map/finish_input/pallas_call | solution.py:54
  (343 shorter events, 157.3 us)
Async XLA Ops:
  7.2 101.1 %all-gather.9.cloned.1.call-start = ((), (), s32[]{:S(2)}) async-start(), calls=%async_computation.6 | async-start | bytes 3932160 | tf_op jit(solution)/shard_map/all_gather | solution.py:1105
  12.4 173.0 %all-gather.11.cloned.1.call-start = ((), (), s32[]{:S(2)}) async-start(), calls=%async_computation.7 | async-start | bytes 5242880 | tf_op jit(solution)/shard_map/all_gather | solution.py:1105
  15.8 243.8 %all-gather.15.cloned.1.call-start = ((), (), s32[]{:S(2)}) async-start(), calls=%async_computation.9 | async-start | bytes 5242880 | tf_op jit(solution)/shard_map/all_gather | solution.py:1105
  20.7 40.2 %collective-permute-start.10 = (bf16[256,2048]{1,0:T(8,128)(2,1)}, bf16[256,2048]{1,0:T(8,128)(2,1)S(1)}, u32[]{:S(2)}, u32[]{:S(2)}) collective-permute-start(bf16[256,2048]{1,0:T(8,128)(2,1)} %get-tuple-element.77), channel_id=1, source_target_pairs={{0,4},{4,0},{8,12},{12,8},{1,5},{5,1},{9,13},{13,9},{2,6},{6,2},{1... | collective-permute-start | bytes 3145736 | tf_op jit(solution)/shard_map/ppermute | solution.py:93
  24.7 244.9 %all-gather.13.cloned.1.call-start = ((), (), s32[]{:S(2)}) async-start(), calls=%async_computation.8 | async-start | bytes 1310720 | tf_op jit(solution)/shard_map/all_gather | solution.py:1105
  24.9 44.9 %collective-permute-start = (bf16[256,2048]{1,0:T(8,128)(2,1)}, bf16[256,2048]{1,0:T(8,128)(2,1)}, u32[]{:S(2)}, u32[]{:S(2)}) collective-permute-start(bf16[256,2048]{1,0:T(8,128)(2,1)} %get-tuple-element.72), channel_id=1, source_target_pairs={{0,4},{4,0},{8,12},{12,8},{1,5},{5,1},{9,13},{13,9},{2,6},{6,2},{1... | collective-permute-start | bytes 3145736 | tf_op jit(solution)/shard_map/ppermute | solution.py:93
  25.2 44.6 %collective-permute-start.6 = (bf16[256,2048]{1,0:T(8,128)(2,1)}, bf16[256,2048]{1,0:T(8,128)(2,1)S(1)}, u32[]{:S(2)}, u32[]{:S(2)}) collective-permute-start(bf16[256,2048]{1,0:T(8,128)(2,1)} %get-tuple-element.72), channel_id=1, source_target_pairs={{0,8},{4,12},{8,0},{12,4},{1,9},{5,13},{9,1},{13,5},{2,10},{6,14},... | collective-permute-start | bytes 3145736 | tf_op jit(solution)/shard_map/ppermute | solution.py:93
  27.0 46.2 %collective-permute-start.7 = (bf16[256,2048]{1,0:T(8,128)(2,1)}, bf16[256,2048]{1,0:T(8,128)(2,1)S(1)}, u32[]{:S(2)}, u32[]{:S(2)}) collective-permute-start(bf16[256,2048]{1,0:T(8,128)(2,1)} %get-tuple-element.77), channel_id=1, source_target_pairs={{0,8},{4,12},{8,0},{12,4},{1,9},{5,13},{9,1},{13,5},{2,10},{6,14},... | collective-permute-start | bytes 3145736 | tf_op jit(solution)/shard_map/ppermute | solution.py:93
  103.4 41.1 %collective-permute-start.17 = (bf16[256,2048]{1,0:T(8,128)(2,1)}, bf16[256,2048]{1,0:T(8,128)(2,1)}, u32[]{:S(2)}, u32[]{:S(2)}) collective-permute-start(bf16[256,2048]{1,0:T(8,128)(2,1)} %hold.48), channel_id=1, source_target_pairs={{0,8},{4,12},{8,0},{12,4},{1,9},{5,13},{9,1},{13,5},{2,10},{6,14},... | collective-permute-start | bytes 3145736 | tf_op jit(solution)/shard_map/ppermute | solution.py:93
  106.2 38.4 %collective-permute-start.16 = (bf16[256,2048]{1,0:T(8,128)(2,1)}, bf16[256,2048]{1,0:T(8,128)(2,1)S(1)}, u32[]{:S(2)}, u32[]{:S(2)}) collective-permute-start(bf16[256,2048]{1,0:T(8,128)(2,1)} %hold.46), channel_id=1, source_target_pairs={{0,4},{4,0},{8,12},{12,8},{1,5},{5,1},{9,13},{13,9},{2,6},{6,2},{1... | collective-permute-start | bytes 3145736 | tf_op jit(solution)/shard_map/ppermute | solution.py:93
  145.5 37.9 %collective-permute-start.18 = (bf16[256,2048]{1,0:T(8,128)(2,1)}, bf16[256,2048]{1,0:T(8,128)(2,1)S(1)}, u32[]{:S(2)}, u32[]{:S(2)}) collective-permute-start(bf16[256,2048]{1,0:T(8,128)(2,1)} %hold.50), channel_id=1, source_target_pairs={{0,4},{4,0},{8,12},{12,8},{1,5},{5,1},{9,13},{13,9},{2,6},{6,2},{1... | collective-permute-start | bytes 3145736 | tf_op jit(solution)/shard_map/ppermute | solution.py:93
  146.0 38.4 %collective-permute-start.20 = (bf16[256,2048]{1,0:T(8,128)(2,1)}, bf16[256,2048]{1,0:T(8,128)(2,1)S(1)}, u32[]{:S(2)}, u32[]{:S(2)}) collective-permute-start(bf16[256,2048]{1,0:T(8,128)(2,1)} %hold.52), channel_id=1, source_target_pairs={{0,8},{4,12},{8,0},{12,4},{1,9},{5,13},{9,1},{13,5},{2,10},{6,14},... | collective-permute-start | bytes 3145736 | tf_op jit(solution)/shard_map/ppermute | solution.py:93
  146.4 67.6 %collective-permute-start.25 = (bf16[256,2048]{1,0:T(8,128)(2,1)}, bf16[256,2048]{1,0:T(8,128)(2,1)}, u32[]{:S(2)}, u32[]{:S(2)}) collective-permute-start(bf16[256,2048]{1,0:T(8,128)(2,1)} %hold.49.refs_6_.refs_2_), channel_id=1, source_target_pairs={{0,4},{4,0},{8,12},{12,8},{1,5},{5,1},{9,13},{13,9},{2,6},{6,2},{1... | collective-permute-start | bytes 3145736 | tf_op jit(solution)/shard_map/ppermute | solution.py:93
  148.0 66.5 %collective-permute-start.24 = (bf16[256,2048]{1,0:T(8,128)(2,1)S(1)}, bf16[256,2048]{1,0:T(8,128)(2,1)}, u32[]{:S(2)}, u32[]{:S(2)}) collective-permute-start(bf16[256,2048]{1,0:T(8,128)(2,1)S(1)} %copy-done.2), channel_id=1, source_target_pairs={{0,8},{4,12},{8,0},{12,4},{1,9},{5,13},{9,1},{13,5},{2,10},{6,14},... | collective-permute-start | bytes 3145736 | tf_op jit(solution)/shard_map/ppermute | solution.py:93
  149.6 65.0 %collective-permute-start.19 = (bf16[256,2048]{1,0:T(8,128)(2,1)S(1)}, bf16[256,2048]{1,0:T(8,128)(2,1)}, u32[]{:S(2)}, u32[]{:S(2)}) collective-permute-start(bf16[256,2048]{1,0:T(8,128)(2,1)S(1)} %copy-done.2), channel_id=1, source_target_pairs={{0,16},{16,0},{1,17},{17,1},{2,18},{18,2},{3,19},{19,3},{4,20},{20... | collective-permute-start | bytes 3145736 | tf_op jit(solution)/shard_map/ppermute | solution.py:93
  183.4 32.6 %collective-permute-start.23 = (bf16[256,2048]{1,0:T(8,128)(2,1)}, bf16[256,2048]{1,0:T(8,128)(2,1)}, u32[]{:S(2)}, u32[]{:S(2)}) collective-permute-start(bf16[256,2048]{1,0:T(8,128)(2,1)} %hold.49.refs_6_.refs_2_), channel_id=1, source_target_pairs={{0,16},{16,0},{1,17},{17,1},{2,18},{18,2},{3,19},{19,3},{4,20},{20... | collective-permute-start | bytes 3145736 | tf_op jit(solution)/shard_map/ppermute | solution.py:93
  184.4 30.6 %collective-permute-start.21 = (bf16[256,2048]{1,0:T(8,128)(2,1)}, bf16[256,2048]{1,0:T(8,128)(2,1)S(1)}, u32[]{:S(2)}, u32[]{:S(2)}) collective-permute-start(bf16[256,2048]{1,0:T(8,128)(2,1)} %hold.51.refs_4_.refs_2_), channel_id=1, source_target_pairs={{0,16},{16,0},{1,17},{17,1},{2,18},{18,2},{3,19},{19,3},{4,20},{20... | collective-permute-start | bytes 3145736 | tf_op jit(solution)/shard_map/ppermute | solution.py:93
  222.3 317.6 %reduce-scatter.6.cloned.1.call-start = ((), (), s32[]{:S(2)}) async-start(), calls=%async_computation.4 | async-start | bytes 5242880 | tf_op jit(solution)/shard_map/reduce_scatter | solution.py:1182
  259.4 285.6 %reduce-scatter.4.cloned.1.call-start = ((), (), s32[]{:S(2)}) async-start(), calls=%async_computation.3 | async-start | bytes 5242880 | tf_op jit(solution)/shard_map/reduce_scatter | solution.py:1182
  259.5 61.1 %collective-permute-start.27 = (bf16[2048,1024]{1,0:T(8,128)(2,1)}, bf16[2048,1024]{1,0:T(8,128)(2,1)}, u32[]{:S(2)}, u32[]{:S(2)}) collective-permute-start(bf16[2048,1024]{1,0:T(8,128)(2,1)} %hold.61), channel_id=1, source_target_pairs={{0,16},{16,0},{1,17},{17,1},{2,18},{18,2},{3,19},{19,3},{4,20},{20... | collective-permute-start | bytes 12582920 | tf_op jit(solution)/shard_map/ppermute | solution.py:93
  259.6 60.9 %collective-permute-start.31 = (bf16[4,2,1024,256]{3,2,1,0:T(8,128)(2,1)}, bf16[4,2,1024,256]{3,2,1,0:T(8,128)(2,1)}, u32[]{:S(2)}, u32[]{:S(2)}) collective-permute-start(bf16[4,2,1024,256]{3,2,1,0:T(8,128)(2,1)} %hold.62.refs_2_.refs_6_), channel_id=1, source_target_pairs={{0,16},{16,0},{1,17},{17,1},{2,18},{18,2},{3,19},{19,3},{4,20},{20... | collective-permute-start | bytes 12582920 | tf_op jit(solution)/shard_map/ppermute | solution.py:93
  269.6 50.9 %collective-permute-start.28 = (bf16[4,2,256,256]{3,2,1,0:T(8,128)(2,1)}, bf16[4,2,256,256]{3,2,1,0:T(8,128)(2,1)S(1)}, u32[]{:S(2)}, u32[]{:S(2)}) collective-permute-start(bf16[4,2,256,256]{3,2,1,0:T(8,128)(2,1)} %bitcast.100), channel_id=1, source_target_pairs={{0,16},{16,0},{1,17},{17,1},{2,18},{18,2},{3,19},{19,3},{4,20},{20... | collective-permute-start | bytes 3145736 | tf_op jit(solution)/shard_map/ppermute | solution.py:93
  269.6 50.9 %collective-permute-start.26 = (bf16[2048,256]{1,0:T(8,128)(2,1)}, bf16[2048,256]{1,0:T(8,128)(2,1)S(1)}, u32[]{:S(2)}, u32[]{:S(2)}) collective-permute-start(bf16[2048,256]{1,0:T(8,128)(2,1)} %hold.60), channel_id=1, source_target_pairs={{0,16},{16,0},{1,17},{17,1},{2,18},{18,2},{3,19},{19,3},{4,20},{20... | collective-permute-start | bytes 3145736 | tf_op jit(solution)/shard_map/ppermute | solution.py:93
  382.1 56.0 %collective-permute-start.35 = (bf16[512,2048]{1,0:T(8,128)(2,1)}, bf16[512,2048]{1,0:T(8,128)(2,1)}, u32[]{:S(2)}, u32[]{:S(2)}) collective-permute-start(bf16[512,2048]{1,0:T(8,128)(2,1)} %output_piece.7.refs_11_.refs_12_), channel_id=1, source_target_pairs={{0,8},{4,12},{8,0},{12,4},{1,9},{5,13},{9,1},{13,5},{2,10},{6,14},... | collective-permute-start | bytes 6291464 | tf_op jit(solution)/shard_map/ppermute | solution.py:93
  382.7 55.4 %collective-permute-start.34 = (bf16[512,2048]{1,0:T(8,128)(2,1)}, bf16[512,2048]{1,0:T(8,128)(2,1)}, u32[]{:S(2)}, u32[]{:S(2)}) collective-permute-start(bf16[512,2048]{1,0:T(8,128)(2,1)} %output_piece.6.refs_9_.refs_10_), channel_id=1, source_target_pairs={{0,4},{4,0},{8,12},{12,8},{1,5},{5,1},{9,13},{13,9},{2,6},{6,2},{1... | collective-permute-start | bytes 6291464 | tf_op jit(solution)/shard_map/ppermute | solution.py:93
  383.4 203.7 %reduce-scatter.8.cloned.1.call-start = ((), (), s32[]{:S(2)}) async-start(), calls=%async_computation.5 | async-start | bytes 5242880 | tf_op jit(solution)/shard_map/reduce_scatter | solution.py:1182
  383.4 55.2 %collective-permute-start.39 = (bf16[4,2,256,1024]{3,2,1,0:T(8,128)(2,1)}, bf16[4,2,256,1024]{3,2,1,0:T(8,128)(2,1)}, u32[]{:S(2)}, u32[]{:S(2)}) collective-permute-start(bf16[4,2,256,1024]{3,2,1,0:T(8,128)(2,1)} %bitcast.76), channel_id=1, source_target_pairs={{0,16},{16,0},{1,17},{17,1},{2,18},{18,2},{3,19},{19,3},{4,20},{20... | collective-permute-start | bytes 12582920 | tf_op jit(solution)/shard_map/ppermute | solution.py:93
  383.5 55.2 %collective-permute-start.37 = (bf16[2048,1024]{1,0:T(8,128)(2,1)}, bf16[2048,1024]{1,0:T(8,128)(2,1)}, u32[]{:S(2)}, u32[]{:S(2)}) collective-permute-start(bf16[2048,1024]{1,0:T(8,128)(2,1)} %get-tuple-element.111), channel_id=1, source_target_pairs={{0,16},{16,0},{1,17},{17,1},{2,18},{18,2},{3,19},{19,3},{4,20},{20... | collective-permute-start | bytes 12582920 | tf_op jit(solution)/shard_map/ppermute | solution.py:93
  384.0 54.7 %collective-permute-start.38 = (bf16[4,2,256,768]{3,2,1,0:T(8,128)(2,1)S(1)}, bf16[4,2,256,768]{3,2,1,0:T(8,128)(2,1)}, u32[]{:S(2)}, u32[]{:S(2)}) collective-permute-start(bf16[4,2,256,768]{3,2,1,0:T(8,128)(2,1)S(1)} %bitcast.74), channel_id=1, source_target_pairs={{0,16},{16,0},{1,17},{17,1},{2,18},{18,2},{3,19},{19,3},{4,20},{20... | collective-permute-start | bytes 9437192 | tf_op jit(solution)/shard_map/ppermute | solution.py:93
  516.1 56.8 %collective-permute-start.46 = (bf16[512,2048]{1,0:T(8,128)(2,1)}, bf16[512,2048]{1,0:T(8,128)(2,1)}, u32[]{:S(2)}, u32[]{:S(2)}) collective-permute-start(bf16[512,2048]{1,0:T(8,128)(2,1)} %get-tuple-element.120.refs_12_), channel_id=1, source_target_pairs={{0,8},{4,12},{8,0},{12,4},{1,9},{5,13},{9,1},{13,5},{2,10},{6,14},... | collective-permute-start | bytes 6291464 | tf_op jit(solution)/shard_map/ppermute | solution.py:93
  517.4 55.5 %collective-permute-start.45 = (bf16[512,2048]{1,0:T(8,128)(2,1)}, bf16[512,2048]{1,0:T(8,128)(2,1)S(1)}, u32[]{:S(2)}, u32[]{:S(2)}) collective-permute-start(bf16[512,2048]{1,0:T(8,128)(2,1)} %get-tuple-element.118.refs_13_), channel_id=1, source_target_pairs={{0,4},{4,0},{8,12},{12,8},{1,5},{5,1},{9,13},{13,9},{2,6},{6,2},{1... | collective-permute-start | bytes 6291464 | tf_op jit(solution)/shard_map/ppermute | solution.py:93
  539.8 41.9 %collective-permute-start.42 = (bf16[512,2048]{1,0:T(8,128)(2,1)}, bf16[512,2048]{1,0:T(8,128)(2,1)}, u32[]{:S(2)}, u32[]{:S(2)}) collective-permute-start(bf16[512,2048]{1,0:T(8,128)(2,1)} %get-tuple-element.122.refs_2_.refs_1_), channel_id=1, source_target_pairs={{0,16},{16,0},{1,17},{17,1},{2,18},{18,2},{3,19},{19,3},{4,20},{20... | collective-permute-start | bytes 6291464 | tf_op jit(solution)/shard_map/ppermute | solution.py:93
  (87 other events, 632.7 us)
Sparse Core Ops, SparseCore 0:
  12.5 66.1 all-gather.8
  80.8 79.3 all-gather.10
  161.8 79.2 all-gather.14
  243.1 26.4 all-gather.12
  271.8 76.2 reduce-scatter.5
  383.5 75.8 reduce-scatter.3
  489.2 77.2 reduce-scatter.7
where the time goes:
time: 634 us; the launch traced here: 623 us
  Pallas kernels  392 us (62%)
  matrix products  63.9 us (10%)
  waiting for transfers between devices  52.5 us (8%)
  local copies, waits for them, and re-layouts  39.5 us (6%)
  starting transfers between devices  39 us (6%)
  other arithmetic  20.6 us (3%)
  between operations  15.2 us (2%)
    pallas_call x76, Pallas kernels, launch(): pl.pallas_call(body, grid_spec=pltpu.PrefetchScalarGridSpec(num_scalar_pr...  392 us
    dot_general x3, matrix products, weight_grad(): lax.dot_general(left, right, CONTRACT_FIRST, preferred_element_type=F32)  63.9 us
    ppermute x55, waiting for transfers between devices, swap(): return lax.ppermute(value, axis, [(i, i ^ bit) for i in range(size)])  42.8 us
    ppermute x55, starting transfers between devices, swap(): return lax.ppermute(value, axis, [(i, i ^ bit) for i in range(size)])  38.7 us
    unnamed x119, local copies, waits for them, and re-layouts  28.8 us
  transfers between devices with their start and end apart: 62, of which 15 were waited for; matrix products, arithmetic and copies ran while one was open for 15% of the time, Pallas kernels for 61%

commit v1 on v0

--- a/solution.py
+++ b/solution.py
@@ -803,13 +803,13 @@
     @pl.when(step == pl.num_programs(0) - 1)
     def _():
         for z, c, at in chunks_of(dense):
-            blocks[z, c] = total[:, at * share : (at + 1) * share].T.astype(BF16)
+            blocks[c, z] = total[:, at * share : (at + 1) * share].T.astype(BF16)
 
 
 def dense_back(grad, attended, dense, tokens):
     rows, width = grad.shape
     groups, cores, cols, share = dense.shape
-    turned = jax.ShapeDtypeStruct((groups, cores, share, cols), BF16)
+    turned = jax.ShapeDtypeStruct((cores, groups, share, cols), BF16)
     tile = 512
     return launch(
         dense_back_kernel,
@@ -1176,10 +1176,10 @@
         return lax.dot_general(left, right, CONTRACT_FIRST, preferred_element_type=F32).astype(BF16)
 
     def in_order(part):
-        return part.reshape(2, groups, share, part.shape[1]).transpose(1, 0, 2, 3)
+        return part.reshape(2, groups, share, part.shape[1])
 
     def scatter(blocks):
-        return lax.psum_scatter(blocks, "seq", scatter_dimension=0, tiled=False)
+        return lax.psum_scatter(blocks, "seq", scatter_dimension=1, tiled=False)
 
     def exchanged(own, send, *tokens):
         send = send.reshape(-1, send.shape[-1])
@@ -1188,8 +1188,6 @@
     def with_other_weight(weight):
         return weight, swap(weight, "branch", 1)
 
-    attended_pair = exchanged(attended, attended_send, *arrived)
-    activated_pair = exchanged(activated, activated_send, *arrived)
     contract_blocks = in_order(weight_grad(grad_rows, activated))
     contract_total = scatter(contract_blocks)
     contract_full = hold(contract_full, contract_blocks)
@@ -1197,7 +1195,10 @@
         grad_rows, slope, contract_full, [contract_blocks]
     )
     pre_pair = exchanged(pre_grad, pre_send)
-    contract_pair = with_other_weight(contract_full)
+    dense_full = hold(dense_full, pre_sums)
+    attended_pair = exchanged(attended, attended_send, pre_sums)
+    activated_pair = exchanged(activated, activated_send, pre_sums)
+    contract_pair = with_other_weight(hold(contract_full, pre_sums))
     expand_blocks = in_order(weight_grad(second_normed, pre_grad))
     expand_total = scatter(expand_blocks)
     dense_pair = with_other_weight(dense_full)
@@ -1285,20 +1286,30 @@
     def output_body(values, whole):
         return add_up(values) + whole[0][...] + whole[1][...]
 
+    def input_body(values, whole):
+        x, grad = values[0].astype(F32), values[1].astype(F32)
+        total = add_up(values[2:])
+        centred = x - jnp.mean(x, axis=-1, keepdims=True)
+        rate = lax.rsqrt(jnp.mean(centred * centred, axis=-1, keepdims=True) + EPSILON)
+        n = centred * rate
+        middle = jnp.mean(total, axis=-1, keepdims=True)
+        along = jnp.mean(total * n, axis=-1, keepdims=True)
+        return grad + rate * (total - middle - n * along)
+
     def all_sum_beside(value, axis, others):
         size = lax.axis_size(axis)
         bit = 1
         while bit < size:
             arrived = swap(value, axis, bit)
             if others:
-                arrived = hold(arrived, *others.pop(0)())
+                arrived = hold(arrived, *others.pop(0)(value))
             value = value + arrived
             bit *= 2
         return value
 
     kept = {}
 
-    def first_beside():
+    def first_beside(value):
         kept["both"], kept["own"] = finish_tile(
             output_body,
             "finish_output",
@@ -1307,36 +1318,37 @@
             biases,
             tile,
             model_width,
-            [mark],
+            [value],
         )
         return [kept["own"]]
 
-    def second_beside():
-        kept["contract"] = pick_other(place, contract_total, [kept["own"]])
-        kept["expand"] = pick_other(place, expand_total, [kept["contract"]])
-        return [kept["expand"]]
-
-    def third_beside():
-        (kept["contract_grad"],) = join_cores(
-            place, contract_total, kept["contract"], 0, [kept["expand"]]
+    def second_beside(value):
+        kept["contract"] = pick_other(place, contract_total, [value])
+        return [kept["contract"]]
+
+    def third_beside(value):
+        kept["expand"] = pick_other(place, expand_total, [value, kept["contract"]])
+        return [kept["expand"], *landed]
+
+    def fourth_beside(value):
+        kept["input_both"], kept["input_own"] = finish_tile(
+            input_body,
+            "finish_input",
+            place,
+            [block_input, output_grad] + inputs.terms(),
+            (),
+            tile,
+            model_width,
+            [value],
         )
-        return [kept["contract_grad"], *landed]
-
-    def fourth_beside():
+        return [kept["input_own"]]
+
+    def fifth_beside(value):
+        (kept["contract_grad"],) = join_cores(place, contract_total, kept["contract"], 0, [value])
         (kept["expand_grad"],) = join_cores(
-            place,
-            expand_total,
-            kept["expand"],
-            expand_total.shape[2],
-            [kept["contract_grad"]],
+            place, expand_total, kept["expand"], expand_total.shape[2], [kept["contract_grad"]]
         )
         return [kept["expand_grad"]]
-
-    def fifth_beside():
-        kept["output"] = fill_other(
-            place, kept["both"], swap(kept["own"], "branch", 1), [kept["expand_grad"]]
-        )
-        return [kept["output"]]
 
     others = [first_beside, second_beside, third_beside, fourth_beside, fifth_beside]
     joined_bias_part = jnp.sum(joined_sums, axis=0).reshape(-1)
@@ -1359,36 +1371,17 @@
     shared = all_sum_beside(small[:everywhere], "tp", others)
     shared = all_sum_beside(shared, "branch", others).reshape(5, model_width)
     while others:
-        others.pop(0)()
-    block_output, contract_grad = kept["output"], kept["contract_grad"]
-    expand_grad = kept["expand_grad"]
-    joined_other = pick_other(place, joined_total, [shared, block_output])
-
-    def input_body(values, whole):
-        x, grad = values[0].astype(F32), values[1].astype(F32)
-        total = add_up(values[2:])
-        centred = x - jnp.mean(x, axis=-1, keepdims=True)
-        rate = lax.rsqrt(jnp.mean(centred * centred, axis=-1, keepdims=True) + EPSILON)
-        n = centred * rate
-        middle = jnp.mean(total, axis=-1, keepdims=True)
-        along = jnp.mean(total * n, axis=-1, keepdims=True)
-        return grad + rate * (total - middle - n * along)
-
-    input_both, input_grad_own = finish_tile(
-        input_body,
-        "finish_input",
-        place,
-        [block_input, output_grad] + inputs.terms(),
-        (),
-        tile,
-        model_width,
-        [joined_other],
+        others.pop(0)(mark)
+    contract_grad, expand_grad = kept["contract_grad"], kept["expand_grad"]
+    block_output = fill_other(
+        place, kept["both"], swap(kept["own"], "branch", 1), [expand_grad]
+    )
+    joined_other = pick_other(place, joined_total, [block_output])
+    input_grad = fill_other(
+        place, kept["input_both"], swap(kept["input_own"], "branch", 1), [joined_other]
     )
     query_key_value_grad, dense_grad = join_cores(
-        place, joined_total, joined_other, joined_weight.shape[3], [input_grad_own]
-    )
-    input_grad = fill_other(
-        place, input_both, swap(input_grad_own, "branch", 1), [query_key_value_grad]
+        place, joined_total, joined_other, joined_weight.shape[3], [input_grad]
     )
     return (
         block_output,

time: 634 us -> 646 us (1.019)
  Pallas kernels: 392 us -> 412 us
  waiting for transfers between devices: 52.5 us -> 41.8 us
  starting transfers between devices: 39 us -> 30.5 us
  local copies, waits for them, and re-layouts: 39.5 us -> 46.9 us
    pallas_call x76 -> x78, Pallas kernels: 392 us -> 412 us  [launch(): pl.pallas_call(body, grid_spec=pltpu.PrefetchScalarGridSpec(num_scalar_pr...]
    all_gather x4, waiting for transfers between devices: 9.59 us -> 0.02 us  [gather_seq(): return lax.all_gather(piece, 'seq', axis=0)]
    ppermute x55, starting transfers between devices: 38.7 us -> 30.2 us  [swap(): return lax.ppermute(value, axis, [(i, i ^ bit) for i in range(size)])]
    unnamed x119 -> x133, local copies, waits for them, and re-layouts: 28.8 us -> 35.7 us
  transfers between devices with their start and end apart: 62 -> 62, of which waited for: 15 -> 13; matrix products, arithmetic and copies ran while one was open for 15% -> 16% of each run, Pallas kernels for 61% -> 64%
where the time goes in v1:
time: 646 us; the launch traced here: 635 us
  Pallas kernels  412 us (64%)
  matrix products  65 us (10%)
  local copies, waits for them, and re-layouts  46.9 us (7%)
  waiting for transfers between devices  41.8 us (6%)
  starting transfers between devices  30.5 us (5%)
  other arithmetic  23.1 us (4%)
  between operations  15 us (2%)
    pallas_call x78, Pallas kernels, launch(): pl.pallas_call(body, grid_spec=pltpu.PrefetchScalarGridSpec(num_scalar_pr...  412 us
    dot_general x3, matrix products, weight_grad(): lax.dot_general(left, right, CONTRACT_FIRST, preferred_element_type=F32)  65 us
    ppermute x55, waiting for transfers between devices, swap(): return lax.ppermute(value, axis, [(i, i ^ bit) for i in range(size)])  41.7 us
    unnamed x133, local copies, waits for them, and re-layouts  35.7 us
    ppermute x55, starting transfers between devices, swap(): return lax.ppermute(value, axis, [(i, i ^ bit) for i in range(size)])  30.2 us
  transfers between devices with their start and end apart: 62, of which 13 were waited for; matrix products, arithmetic and copies ran while one was open for 16% of the time, Pallas kernels for 64%

profile of v1, /device:TPU:0, one launch (start us, length us, event | category | flops | bytes accessed | tf_op | source)
XLA Modules:
  0.0 634.7 jit_solution(3919095028912637539)
XLA Ops:
  31.3 10.8 %rotary_tables.1 = (f32[4096,128]{1,0:T(8,128)}, f32[4096,128]{1,0:T(8,128)}, f32[4096,128]{1,0:T(8,128)}) custom-call(s32[2]{0:T(128)} %pad_add_fusion.refs_0_, s32[2,8]{1,0:T(2,128)} %refs_1_.15, bf16[2,256,768]{2,1,0:T(8,128)(2,1)} %pad_maximum_fusion.3.refs_2_, bf16[2,256,1024]{2,1,0:T(8,128)(2,1)} %pad_maximum_fusion.1.refs_3_, ...), custom_call_target="tpu_custom_call" | custom-call | flops 1048577 | bytes 503317 | tf_op jit(solution)/shard_map/rotary_tables/pallas_call | solution.py:54
  45.8 5.4 place_piece.4.refs_10_.refs_5_
  51.2 9.6 %norm_piece.4 = (bf16[4096,2048]{1,0:T(8,128)(2,1)}, bf16[4096,2048]{1,0:T(8,128)(2,1)}, bf16[4096,2048]{1,0:T(8,128)(2,1)}, f32[8,128]{1,0:T(8,128)}) custom-call(s32[2]{0:T(128)} %pad_add_fusion.refs_0_, bf16[2,512,2048]{2,1,0:T(8,128)(2,1)} %refs_1_.17, bf16[2,512,2048]{2,1,0:T(8,128)(2,1)} %refs_1_.17, bf16[2,512,2048]{2,1,0:T(8,128)(2,1)} %refs_1_.17, ...), custom_call_target="tpu_custom_call" | custom-call | flops 671089 | bytes 671089 | tf_op jit(solution)/shard_map/norm_piece/pallas_call | solution.py:54
  61.8 8.0 %collective-permute-done.10.refs_0_ = bf16[256,2048]{1,0:T(8,128)(2,1)} collective-permute-done((bf16[256,2048]{1,0:T(8,128)(2,1)}, bf16[256,2048]{1,0:T(8,128)(2,1)}, u32[]{:S(2)}, u32[]{:S(2)}) %collective-permute-start.10) | collective-permute-done | bytes 1048608 | tf_op jit(solution)/shard_map/ppermute | solution.py:93
  77.1 9.5 %norm_piece.5 = (bf16[4096,2048]{1,0:T(8,128)(2,1)}, bf16[4096,2048]{1,0:T(8,128)(2,1)}, bf16[4096,2048]{1,0:T(8,128)(2,1)}, f32[8,128]{1,0:T(8,128)}) custom-call(s32[2]{0:T(128)} %pad_add_fusion.refs_0_, bf16[256,2048]{1,0:T(8,128)(2,1)} %hold.42.refs_1_, ...), custom_call_target="tpu_custom_call", output_to_operand_aliasing={{0}: (9, {}), {1}: (10, {}), {2}: (11, {})} | custom-call | flops 671089 | bytes 671089 | tf_op jit(solution)/shard_map/norm_piece/pallas_call | solution.py:54
  87.9 9.7 %norm_piece.6 = (bf16[4096,2048]{1,0:T(8,128)(2,1)}, bf16[4096,2048]{1,0:T(8,128)(2,1)}, bf16[4096,2048]{1,0:T(8,128)(2,1)}, f32[8,128]{1,0:T(8,128)}) custom-call(s32[2]{0:T(128)} %pad_add_fusion.refs_0_, bf16[256,2048]{1,0:T(8,128)(2,1)} %hold.43.refs_1_, ...), custom_call_target="tpu_custom_call", output_to_operand_aliasing={{0}: (9, {}), {1}: (10, {}), {2}: (11, {})} | custom-call | flops 671089 | bytes 671089 | tf_op jit(solution)/shard_map/norm_piece/pallas_call | solution.py:54
  106.8 16.9 %project.2 = (bf16[2,2,4,512,128]{4,3,2,1,0:T(8,128)(2,1)}, bf16[2,2,4,512,128]{4,3,2,1,0:T(8,128)(2,1)}, bf16[2,2,4,512,128]{4,3,2,1,0:T(8,128)(2,1)}) custom-call(bf16[4096,2048]{1,0:T(8,128)(2,1)} %get-tuple-element.86.refs_0_.refs_10_, bf16[4,2,256,768]{3,2,1,0:T(8,128)(2,1)} %bitcast.59, f32[1,768]{1,0:T(1,128)} %reshape.104.refs_2_, ...), custom_call_target="tpu_custom_call" | custom-call | flops 193273536 | bytes 408945 | tf_op jit(solution)/shard_map/project/pallas_call | solution.py:54
  124.7 9.7 %norm_piece.7 = (bf16[4096,2048]{1,0:T(8,128)(2,1)}, bf16[4096,2048]{1,0:T(8,128)(2,1)}, bf16[4096,2048]{1,0:T(8,128)(2,1)}, f32[8,128]{1,0:T(8,128)}) custom-call(s32[2]{0:T(128)} %pad_add_fusion.refs_0_, bf16[256,2048]{1,0:T(8,128)(2,1)} %hold.46.refs_1_, ...), custom_call_target="tpu_custom_call", output_to_operand_aliasing={{0}: (9, {}), {1}: (10, {}), {2}: (11, {})} | custom-call | flops 671089 | bytes 671089 | tf_op jit(solution)/shard_map/norm_piece/pallas_call | solution.py:54
  134.4 8.4 %project.3 = (bf16[2,2,4,512,128]{4,3,2,1,0:T(8,128)(2,1)}, bf16[2,2,4,512,128]{4,3,2,1,0:T(8,128)(2,1)}, bf16[2,2,4,512,128]{4,3,2,1,0:T(8,128)(2,1)}) custom-call(bf16[4096,2048]{1,0:T(8,128)(2,1)} %get-tuple-element.91.refs_0_, bf16[4,2,256,768]{3,2,1,0:T(8,128)(2,1)} %bitcast.60, ...), custom_call_target="tpu_custom_call", output_to_operand_aliasing={{0}: (6, {}), {1}: (7, {}), {2}: (8, {})} | custom-call | flops 64424512 | bytes 178258 | tf_op jit(solution)/shard_map/project/pallas_call | solution.py:54
  148.6 35.8 %attend.1 = (bf16[2,4,512,256]{3,2,1,0:T(8,128)(2,1)}, bf16[4,512,256]{2,1,0:T(8,128)(2,1)}, f32[2,2,4,1,512]{4,3,2,1,0:T(1,128)}) custom-call(s32[2]{0:T(128)} %pad_add_fusion.refs_0_, s32[2,8]{1,0:T(2,128)} %refs_1_.15, bf16[2,2,4,512,128]{4,3,2,1,0:T(8,128)(2,1)} %get-tuple-element.94.refs_1_.refs_2_, ...), custom_call_target="tpu_custom_call" | custom-call | flops 805306368 | bytes 167773 | tf_op jit(solution)/shard_map/attend/pallas_call | solution.py:54
  186.3 28.4 %expand.1 = (bf16[4096,1024]{1,0:T(8,128)(2,1)}, bf16[2048,1024]{1,0:T(8,128)(2,1)}, bf16[4096,1024]{1,0:T(8,128)(2,1)}) custom-call(bf16[4096,2048]{1,0:T(8,128)(2,1)} %get-tuple-element.99.refs_0_, bf16[4,2,256,1024]{3,2,1,0:T(8,128)(2,1)} %bitcast.66, f32[1,1024]{1,0:T(1,128)} %bitcast.131, bf16[256,2048]{1,0:T(8,128)(2,1)} %hold.49.refs_5_.refs_1_.refs_3_, ...), custom_call_target="tpu_custom_call" | custom-call | flops 343597376 | bytes 754975 | tf_op jit(solution)/shard_map/expand/pallas_call | solution.py:54
  223.3 5.4 place_piece.6.refs_5_
  229.6 5.4 place_piece.7.refs_0_
  235.1 22.7 %convolution_convert_fusion.1 = bf16[2048,1024]{1,0:T(8,128)(2,1)S(1)} fusion(bf16[4096,2048]{1,0:T(8,128)(2,1)} %place_piece.7.refs_0_, bf16[4096,1024]{1,0:T(8,128)(2,1)} %get-tuple-element.102.refs_2_), kind=kOutput, calls=%fused_computation.3 | convolution fusion | flops 17181966336 | bytes 29360128 | tf_op jit(solution)/shard_map/dot_general | solution.py:1176
  262.3 37.4 %pre_grad.1 = (bf16[4096,1024]{1,0:T(8,128)(2,1)}, bf16[2048,1024]{1,0:T(8,128)(2,1)}, f32[1,1024]{1,0:T(1,128)}) custom-call(bf16[4096,2048]{1,0:T(8,128)(2,1)} %place_piece.7.refs_0_, bf16[4096,1024]{1,0:T(8,128)(2,1)} %get-tuple-element.101.refs_1_.refs_6_, bf16[4,2,1024,256]{3,2,1,0:T(8,128)(2,1)} %hold.62.refs_2_.refs_0_, bf16[2,4,256,1024]{3,2,1,0:T(8,128)(2,1)} %bitcast.88), custom_call_target="tpu_custom_call" | custom-call | flops 343597376 | bytes 754975 | tf_op jit(solution)/shard_map/pre_grad/pallas_call | solution.py:54
  300.7 23.7 %convolution_convert_fusion = bf16[2048,1024]{1,0:T(8,128)(2,1)} fusion(bf16[4096,2048]{1,0:T(8,128)(2,1)} %get-tuple-element.99.refs_0_, bf16[4096,1024]{1,0:T(8,128)(2,1)} %get-tuple-element.105.refs_2_), kind=kOutput, calls=%fused_computation.2 | convolution fusion | flops 17181966336 | bytes 29360128 | tf_op jit(solution)/shard_map/dot_general | solution.py:1176
  325.8 9.8 %output_piece.4 = (bf16[256,2048]{1,0:T(8,128)(2,1)}, bf16[256,2048]{1,0:T(8,128)(2,1)}) custom-call(bf16[4096,256]{1,0:T(8,128)(2,1)} %bitcast.79, bf16[2048,256]{1,0:T(8,128)(2,1)} %copy-done.10, bf16[4096,1024]{1,0:T(8,128)(2,1)} %get-tuple-element.102.refs_2_, bf16[2048,1024]{1,0:T(8,128)(2,1)} %collective-permute-done.29.refs_3_, ...), custom_call_target="tpu_custom_call" | custom-call | flops 214748368 | bytes 419431 | tf_op jit(solution)/shard_map/output_piece/pallas_call | solution.py:54
  337.0 15.3 %dense_back.1 = (bf16[4096,256]{1,0:T(8,128)(2,1)}, bf16[2,4,256,256]{3,2,1,0:T(8,128)(2,1)}) custom-call(bf16[4096,2048]{1,0:T(8,128)(2,1)} %place_piece.7.refs_0_, bf16[4096,256]{1,0:T(8,128)(2,1)} %bitcast.80, bf16[4,2,256,256]{3,2,1,0:T(8,128)(2,1)} %hold.65.refs_4_.refs_2_, bf16[256,2048]{1,0:T(8,128)(2,1)} %get-tuple-element.106.refs_3_.refs_4_, ...), custom_call_target="tpu_custom_call" | custom-call | flops 171798688 | bytes 398459 | tf_op jit(solution)/shard_map/dense_back/pallas_call | solution.py:54
  352.3 10.0 %output_piece.5.refs_1_.refs_9_.refs_2_ = bf16[512,2048]{1,0:T(8,128)(2,1)} custom-call(bf16[4096,256]{1,0:T(8,128)(2,1)} %bitcast.81, bf16[2048,256]{1,0:T(8,128)(2,1)} %copy-done.10, bf16[4096,1024]{1,0:T(8,128)(2,1)} %get-tuple-element.102.refs_2_, bf16[2048,1024]{1,0:T(8,128)(2,1)} %collective-permute-done.29.refs_3_, ...), custom_call_target="tpu_custom_call" | custom-call | flops 214748368 | bytes 419431 | tf_op jit(solution)/shard_map/output_piece/pallas_call | solution.py:54
  364.3 10.1 %output_piece.6.refs_9_.refs_10_ = bf16[512,2048]{1,0:T(8,128)(2,1)} custom-call(bf16[4096,256]{1,0:T(8,128)(2,1)} %bitcast.82, bf16[2048,256]{1,0:T(8,128)(2,1)} %copy-done.10, bf16[4096,1024]{1,0:T(8,128)(2,1)} %get-tuple-element.102.refs_2_, bf16[2048,1024]{1,0:T(8,128)(2,1)} %collective-permute-done.29.refs_3_, ...), custom_call_target="tpu_custom_call" | custom-call | flops 214748368 | bytes 419431 | tf_op jit(solution)/shard_map/output_piece/pallas_call | solution.py:54
  375.1 10.5 %output_piece.7.refs_11_.refs_12_ = bf16[512,2048]{1,0:T(8,128)(2,1)} custom-call(bf16[4096,256]{1,0:T(8,128)(2,1)} %bitcast.83, bf16[2048,256]{1,0:T(8,128)(2,1)} %copy-done.10, bf16[4096,1024]{1,0:T(8,128)(2,1)} %get-tuple-element.102.refs_2_, bf16[2048,1024]{1,0:T(8,128)(2,1)} %collective-permute-done.29.refs_3_, ...), custom_call_target="tpu_custom_call" | custom-call | flops 214748368 | bytes 419431 | tf_op jit(solution)/shard_map/output_piece/pallas_call | solution.py:54
  391.8 58.2 %attend_back.1 = (bf16[2,4,512,768]{3,2,1,0:T(8,128)(2,1)}, bf16[4,512,768]{2,1,0:T(8,128)(2,1)}, f32[2,1,768]{2,1,0:T(1,128)}) custom-call(s32[2]{0:T(128)} %pad_add_fusion.refs_0_, s32[2,8]{1,0:T(2,128)} %refs_1_.15, bf16[2,2,4,512,128]{4,3,2,1,0:T(8,128)(2,1)} %get-tuple-element.94.refs_1_.refs_2_, ...), custom_call_target="tpu_custom_call" | custom-call | flops 1342177280 | bytes 503317 | tf_op jit(solution)/shard_map/attend_back/pallas_call | solution.py:54
  450.6 5.6 collective-permute-done.36.refs_1_
  456.2 13.2 %normed_grad_piece.4 = (bf16[256,2048]{1,0:T(8,128)(2,1)}, bf16[256,2048]{1,0:T(8,128)(2,1)}, f32[8,2048]{1,0:T(8,128)}) custom-call(bf16[4096,768]{1,0:T(8,128)(2,1)} %bitcast.72, bf16[2048,768]{1,0:T(8,128)(2,1)} %collective-permute-done.36.refs_1_, bf16[4096,1024]{1,0:T(8,128)(2,1)} %get-tuple-element.105.refs_2_, ...), custom_call_target="tpu_custom_call" | custom-call | flops 300647712 | bytes 587203 | tf_op jit(solution)/shard_map/normed_grad_piece/pallas_call | solution.py:54
  470.9 18.5 %convolution_convert_fusion.2.refs_1_.refs_0_ = bf16[2048,768]{1,0:T(8,128)(2,1)} fusion(bf16[4096,2048]{1,0:T(8,128)(2,1)} %hold.72, bf16[4096,768]{1,0:T(8,128)(2,1)S(1)} %bitcast.78), kind=kOutput, calls=%fused_computation.4 | convolution fusion | flops 12886474752 | bytes 26214400 | tf_op jit(solution)/shard_map/dot_general | solution.py:1176
  489.4 5.8 collective-permute-done.41.refs_0_
  505.6 14.2 %normed_grad_piece.5 = (bf16[512,2048]{1,0:T(8,128)(2,1)}, f32[8,2048]{1,0:T(8,128)}) custom-call(bf16[4096,768]{1,0:T(8,128)(2,1)} %bitcast.73, bf16[2048,768]{1,0:T(8,128)(2,1)} %collective-permute-done.36.refs_1_, bf16[4096,1024]{1,0:T(8,128)(2,1)} %get-tuple-element.105.refs_2_, bf16[2048,1024]{1,0:T(8,128)(2,1)} %collective-permute-done.37.refs_3_, ...), custom_call_target="tpu_custom_call" | custom-call | flops 300647712 | bytes 587203 | tf_op jit(solution)/shard_map/normed_grad_piece/pallas_call | solution.py:54
  519.8 13.5 %normed_grad_piece.6 = (bf16[512,2048]{1,0:T(8,128)(2,1)}, f32[8,2048]{1,0:T(8,128)}) custom-call(bf16[4096,768]{1,0:T(8,128)(2,1)} %bitcast.74, bf16[2048,768]{1,0:T(8,128)(2,1)} %collective-permute-done.36.refs_1_, bf16[4096,1024]{1,0:T(8,128)(2,1)} %get-tuple-element.105.refs_2_, bf16[2048,1024]{1,0:T(8,128)(2,1)} %collective-permute-done.37.refs_3_, ...), custom_call_target="tpu_custom_call" | custom-call | flops 300647712 | bytes 587203 | tf_op jit(solution)/shard_map/normed_grad_piece/pallas_call | solution.py:54
  535.9 13.8 %normed_grad_piece.7 = (bf16[512,2048]{1,0:T(8,128)(2,1)}, f32[8,2048]{1,0:T(8,128)}) custom-call(bf16[4096,768]{1,0:T(8,128)(2,1)} %bitcast.75, bf16[2048,768]{1,0:T(8,128)(2,1)} %collective-permute-done.36.refs_1_, bf16[4096,1024]{1,0:T(8,128)(2,1)} %get-tuple-element.105.refs_2_, bf16[2048,1024]{1,0:T(8,128)(2,1)} %collective-permute-done.37.refs_3_, ...), custom_call_target="tpu_custom_call" | custom-call | flops 300647712 | bytes 587203 | tf_op jit(solution)/shard_map/normed_grad_piece/pallas_call | solution.py:54
  552.4 6.4 %finish_output.1 = (bf16[2,512,2048]{2,1,0:T(8,128)(2,1)}, bf16[512,2048]{1,0:T(8,128)(2,1)}) custom-call(s32[2]{0:T(128)} %pad_add_fusion.refs_0_, bf16[2,512,2048]{2,1,0:T(8,128)(2,1)} %refs_1_.17, bf16[512,2048]{1,0:T(8,128)(2,1)} %output_piece.5.refs_1_.refs_9_.refs_2_, bf16[512,2048]{1,0:T(8,128)(2,1)} %hold.69.refs_1_.refs_12_.refs_3_, ...), custom_call_target="tpu_custom_call" | custom-call | flops 419431 | bytes 419431 | tf_op jit(solution)/shard_map/finish_output/pallas_call | solution.py:54
  563.3 10.5 %collective-permute-done.44.refs_0_ = f32[12032]{0:T(1024)S(1)} collective-permute-done((f32[12032]{0:T(1024)}, f32[12032]{0:T(1024)S(1)}, u32[]{:S(2)}, u32[]{:S(2)}) %collective-permute-start.44) | collective-permute-done | bytes 48160 | tf_op jit(solution)/shard_map/ppermute | solution.py:93
  586.8 8.1 %finish_input.1 = (bf16[2,512,2048]{2,1,0:T(8,128)(2,1)}, bf16[512,2048]{1,0:T(8,128)(2,1)}) custom-call(s32[2]{0:T(128)} %pad_add_fusion.refs_0_, bf16[2,512,2048]{2,1,0:T(8,128)(2,1)} %refs_1_.17, bf16[2,512,2048]{2,1,0:T(8,128)(2,1)} %refs_2_.9, bf16[512,2048]{1,0:T(8,128)(2,1)} %get-tuple-element.125.refs_3_, bf16[512,2048]{1,0:T(8,128)(2,1)} %hold.79.refs_2_.refs_4_, ...), custom_call_target="tpu_custom_call" | custom-call | flops 419431 | bytes 419431 | tf_op jit(solution)/shard_map/finish_input/pallas_call | solution.py:54
  (358 shorter events, 149.2 us)
Async XLA Ops:
  7.2 99.6 %all-gather.9.cloned.1.call-start = ((), (), s32[]{:S(2)}) async-start(), calls=%async_computation.6 | async-start | bytes 3932160 | tf_op jit(solution)/shard_map/all_gather | solution.py:1105
  12.4 173.9 %all-gather.11.cloned.1.call-start = ((), (), s32[]{:S(2)}) async-start(), calls=%async_computation.7 | async-start | bytes 5242880 | tf_op jit(solution)/shard_map/all_gather | solution.py:1105
  15.9 246.4 %all-gather.13.cloned.1.call-start = ((), (), s32[]{:S(2)}) async-start(), calls=%async_computation.8 | async-start | bytes 5242880 | tf_op jit(solution)/shard_map/all_gather | solution.py:1105
  20.6 40.2 %collective-permute-start = (bf16[256,2048]{1,0:T(8,128)(2,1)}, bf16[256,2048]{1,0:T(8,128)(2,1)S(1)}, u32[]{:S(2)}, u32[]{:S(2)}) collective-permute-start(bf16[256,2048]{1,0:T(8,128)(2,1)} %get-tuple-element.72), channel_id=1, source_target_pairs={{0,4},{4,0},{8,12},{12,8},{1,5},{5,1},{9,13},{13,9},{2,6},{6,2},{1... | collective-permute-start | bytes 3145736 | tf_op jit(solution)/shard_map/ppermute | solution.py:93
  24.6 275.7 %all-gather.15.cloned.1.call-start = ((), (), s32[]{:S(2)}) async-start(), calls=%async_computation.9 | async-start | bytes 1310720 | tf_op jit(solution)/shard_map/all_gather | solution.py:1105
  24.9 44.9 %collective-permute-start.6 = (bf16[256,2048]{1,0:T(8,128)(2,1)}, bf16[256,2048]{1,0:T(8,128)(2,1)S(1)}, u32[]{:S(2)}, u32[]{:S(2)}) collective-permute-start(bf16[256,2048]{1,0:T(8,128)(2,1)} %get-tuple-element.72), channel_id=1, source_target_pairs={{0,8},{4,12},{8,0},{12,4},{1,9},{5,13},{9,1},{13,5},{2,10},{6,14},... | collective-permute-start | bytes 3145736 | tf_op jit(solution)/shard_map/ppermute | solution.py:93
  26.4 46.7 %collective-permute-start.7 = (bf16[256,2048]{1,0:T(8,128)(2,1)}, bf16[256,2048]{1,0:T(8,128)(2,1)S(1)}, u32[]{:S(2)}, u32[]{:S(2)}) collective-permute-start(bf16[256,2048]{1,0:T(8,128)(2,1)} %get-tuple-element.77), channel_id=1, source_target_pairs={{0,8},{4,12},{8,0},{12,4},{1,9},{5,13},{9,1},{13,5},{2,10},{6,14},... | collective-permute-start | bytes 3145736 | tf_op jit(solution)/shard_map/ppermute | solution.py:93
  26.9 42.9 %collective-permute-start.10 = (bf16[256,2048]{1,0:T(8,128)(2,1)}, bf16[256,2048]{1,0:T(8,128)(2,1)}, u32[]{:S(2)}, u32[]{:S(2)}) collective-permute-start(bf16[256,2048]{1,0:T(8,128)(2,1)} %get-tuple-element.77), channel_id=1, source_target_pairs={{0,4},{4,0},{8,12},{12,8},{1,5},{5,1},{9,13},{13,9},{2,6},{6,2},{1... | collective-permute-start | bytes 3145736 | tf_op jit(solution)/shard_map/ppermute | solution.py:93
  74.0 25.6 %collective-permute-start.5 = (bf16[256,2048]{1,0:T(8,128)(2,1)S(1)}, bf16[256,2048]{1,0:T(8,128)(2,1)S(1)}, u32[]{:S(2)}, u32[]{:S(2)}) collective-permute-start(bf16[256,2048]{1,0:T(8,128)(2,1)S(1)} %copy-done.23), channel_id=1, source_target_pairs={{0,8},{4,12},{8,0},{12,4},{1,9},{5,13},{9,1},{13,5},{2,10},{6,14},... | collective-permute-start | bytes 3145736 | tf_op jit(solution)/shard_map/ppermute | solution.py:93
  103.1 39.8 %collective-permute-start.16 = (bf16[256,2048]{1,0:T(8,128)(2,1)}, bf16[256,2048]{1,0:T(8,128)(2,1)S(1)}, u32[]{:S(2)}, u32[]{:S(2)}) collective-permute-start(bf16[256,2048]{1,0:T(8,128)(2,1)} %hold.48), channel_id=1, source_target_pairs={{0,4},{4,0},{8,12},{12,8},{1,5},{5,1},{9,13},{13,9},{2,6},{6,2},{1... | collective-permute-start | bytes 3145736 | tf_op jit(solution)/shard_map/ppermute | solution.py:93
  104.6 39.2 %collective-permute-start.17 = (bf16[256,2048]{1,0:T(8,128)(2,1)}, bf16[256,2048]{1,0:T(8,128)(2,1)}, u32[]{:S(2)}, u32[]{:S(2)}) collective-permute-start(bf16[256,2048]{1,0:T(8,128)(2,1)} %hold.50), channel_id=1, source_target_pairs={{0,8},{4,12},{8,0},{12,4},{1,9},{5,13},{9,1},{13,5},{2,10},{6,14},... | collective-permute-start | bytes 3145736 | tf_op jit(solution)/shard_map/ppermute | solution.py:93
  143.8 40.5 %collective-permute-start.19 = (bf16[256,2048]{1,0:T(8,128)(2,1)}, bf16[256,2048]{1,0:T(8,128)(2,1)S(1)}, u32[]{:S(2)}, u32[]{:S(2)}) collective-permute-start(bf16[256,2048]{1,0:T(8,128)(2,1)} %hold.52), channel_id=1, source_target_pairs={{0,4},{4,0},{8,12},{12,8},{1,5},{5,1},{9,13},{13,9},{2,6},{6,2},{1... | collective-permute-start | bytes 3145736 | tf_op jit(solution)/shard_map/ppermute | solution.py:93
  145.4 39.9 %collective-permute-start.20 = (bf16[256,2048]{1,0:T(8,128)(2,1)}, bf16[256,2048]{1,0:T(8,128)(2,1)S(1)}, u32[]{:S(2)}, u32[]{:S(2)}) collective-permute-start(bf16[256,2048]{1,0:T(8,128)(2,1)} %hold.54), channel_id=1, source_target_pairs={{0,8},{4,12},{8,0},{12,4},{1,9},{5,13},{9,1},{13,5},{2,10},{6,14},... | collective-permute-start | bytes 3145736 | tf_op jit(solution)/shard_map/ppermute | solution.py:93
  145.9 68.8 %collective-permute-start.18 = (bf16[256,2048]{1,0:T(8,128)(2,1)S(1)}, bf16[256,2048]{1,0:T(8,128)(2,1)}, u32[]{:S(2)}, u32[]{:S(2)}) collective-permute-start(bf16[256,2048]{1,0:T(8,128)(2,1)S(1)} %copy-done.4), channel_id=1, source_target_pairs={{0,8},{4,12},{8,0},{12,4},{1,9},{5,13},{9,1},{13,5},{2,10},{6,14},... | collective-permute-start | bytes 3145736 | tf_op jit(solution)/shard_map/ppermute | solution.py:93
  147.4 67.9 %collective-permute-start.21 = (bf16[256,2048]{1,0:T(8,128)(2,1)}, bf16[256,2048]{1,0:T(8,128)(2,1)}, u32[]{:S(2)}, u32[]{:S(2)}) collective-permute-start(bf16[256,2048]{1,0:T(8,128)(2,1)} %hold.51.refs_6_.refs_2_), channel_id=1, source_target_pairs={{0,4},{4,0},{8,12},{12,8},{1,5},{5,1},{9,13},{13,9},{2,6},{6,2},{1... | collective-permute-start | bytes 3145736 | tf_op jit(solution)/shard_map/ppermute | solution.py:93
  148.0 67.5 %collective-permute-start.26 = (bf16[256,2048]{1,0:T(8,128)(2,1)S(1)}, bf16[256,2048]{1,0:T(8,128)(2,1)}, u32[]{:S(2)}, u32[]{:S(2)}) collective-permute-start(bf16[256,2048]{1,0:T(8,128)(2,1)S(1)} %copy-done.4), channel_id=1, source_target_pairs={{0,16},{16,0},{1,17},{17,1},{2,18},{18,2},{3,19},{19,3},{4,20},{20... | collective-permute-start | bytes 3145736 | tf_op jit(solution)/shard_map/ppermute | solution.py:93
  184.4 32.5 %collective-permute-start.25 = (bf16[256,2048]{1,0:T(8,128)(2,1)}, bf16[256,2048]{1,0:T(8,128)(2,1)}, u32[]{:S(2)}, u32[]{:S(2)}) collective-permute-start(bf16[256,2048]{1,0:T(8,128)(2,1)} %hold.51.refs_6_.refs_2_), channel_id=1, source_target_pairs={{0,16},{16,0},{1,17},{17,1},{2,18},{18,2},{3,19},{19,3},{4,20},{20... | collective-permute-start | bytes 3145736 | tf_op jit(solution)/shard_map/ppermute | solution.py:93
  185.3 30.5 %collective-permute-start.27 = (bf16[256,2048]{1,0:T(8,128)(2,1)}, bf16[256,2048]{1,0:T(8,128)(2,1)S(1)}, u32[]{:S(2)}, u32[]{:S(2)}) collective-permute-start(bf16[256,2048]{1,0:T(8,128)(2,1)} %hold.53.refs_4_.refs_2_), channel_id=1, source_target_pairs={{0,16},{16,0},{1,17},{17,1},{2,18},{18,2},{3,19},{19,3},{4,20},{20... | collective-permute-start | bytes 3145736 | tf_op jit(solution)/shard_map/ppermute | solution.py:93
  223.2 337.6 %reduce-scatter.6.cloned.1.call-start = ((), (), s32[]{:S(2)}) async-start(), calls=%async_computation.4 | async-start | bytes 5242880 | tf_op jit(solution)/shard_map/reduce_scatter | solution.py:1182
  262.2 314.5 %reduce-scatter.4.cloned.1.call-start = ((), (), s32[]{:S(2)}) async-start(), calls=%async_computation.3 | async-start | bytes 5242880 | tf_op jit(solution)/shard_map/reduce_scatter | solution.py:1182
  335.6 26.7 %collective-permute-start.32 = (bf16[256,2048]{1,0:T(8,128)(2,1)}, bf16[256,2048]{1,0:T(8,128)(2,1)S(1)}, u32[]{:S(2)}, u32[]{:S(2)}) collective-permute-start(bf16[256,2048]{1,0:T(8,128)(2,1)} %get-tuple-element.106.refs_3_.refs_4_), channel_id=1, source_target_pairs={{0,8},{4,12},{8,0},{12,4},{1,9},{5,13},{9,1},{13,5},{2,10},{6,14},... | collective-permute-start | bytes 3145736 | tf_op jit(solution)/shard_map/ppermute | solution.py:93
  335.6 27.7 %collective-permute-start.33 = (bf16[256,2048]{1,0:T(8,128)(2,1)}, bf16[256,2048]{1,0:T(8,128)(2,1)S(1)}, u32[]{:S(2)}, u32[]{:S(2)}) collective-permute-start(bf16[256,2048]{1,0:T(8,128)(2,1)} %get-tuple-element.107.refs_5_), channel_id=1, source_target_pairs={{0,4},{4,0},{8,12},{12,8},{1,5},{5,1},{9,13},{13,9},{2,6},{6,2},{1... | collective-permute-start | bytes 3145736 | tf_op jit(solution)/shard_map/ppermute | solution.py:93
  374.4 75.7 %collective-permute-start.34 = (bf16[512,2048]{1,0:T(8,128)(2,1)}, bf16[512,2048]{1,0:T(8,128)(2,1)}, u32[]{:S(2)}, u32[]{:S(2)}) collective-permute-start(bf16[512,2048]{1,0:T(8,128)(2,1)} %output_piece.6.refs_9_.refs_10_), channel_id=1, source_target_pairs={{0,4},{4,0},{8,12},{12,8},{1,5},{5,1},{9,13},{13,9},{2,6},{6,2},{1... | collective-permute-start | bytes 6291464 | tf_op jit(solution)/shard_map/ppermute | solution.py:93
  385.6 64.5 %collective-permute-start.35 = (bf16[512,2048]{1,0:T(8,128)(2,1)}, bf16[512,2048]{1,0:T(8,128)(2,1)}, u32[]{:S(2)}, u32[]{:S(2)}) collective-permute-start(bf16[512,2048]{1,0:T(8,128)(2,1)} %output_piece.7.refs_11_.refs_12_), channel_id=1, source_target_pairs={{0,8},{4,12},{8,0},{12,4},{1,9},{5,13},{9,1},{13,5},{2,10},{6,14},... | collective-permute-start | bytes 6291464 | tf_op jit(solution)/shard_map/ppermute | solution.py:93
  390.0 222.4 %reduce-scatter.8.cloned.1.call-start = ((), (), s32[]{:S(2)}) async-start(), calls=%async_computation.5 | async-start | bytes 5242880 | tf_op jit(solution)/shard_map/reduce_scatter | solution.py:1182
  390.0 60.6 %collective-permute-start.39 = (bf16[4,2,256,1024]{3,2,1,0:T(8,128)(2,1)}, bf16[4,2,256,1024]{3,2,1,0:T(8,128)(2,1)}, u32[]{:S(2)}, u32[]{:S(2)}) collective-permute-start(bf16[4,2,256,1024]{3,2,1,0:T(8,128)(2,1)} %bitcast.67), channel_id=1, source_target_pairs={{0,16},{16,0},{1,17},{17,1},{2,18},{18,2},{3,19},{19,3},{4,20},{20... | collective-permute-start | bytes 12582920 | tf_op jit(solution)/shard_map/ppermute | solution.py:93
  390.1 60.5 %collective-permute-start.37 = (bf16[2048,1024]{1,0:T(8,128)(2,1)}, bf16[2048,1024]{1,0:T(8,128)(2,1)}, u32[]{:S(2)}, u32[]{:S(2)}) collective-permute-start(bf16[2048,1024]{1,0:T(8,128)(2,1)} %get-tuple-element.112), channel_id=1, source_target_pairs={{0,16},{16,0},{1,17},{17,1},{2,18},{18,2},{3,19},{19,3},{4,20},{20... | collective-permute-start | bytes 12582920 | tf_op jit(solution)/shard_map/ppermute | solution.py:93
  391.8 58.7 %collective-permute-start.38 = (bf16[4,2,256,768]{3,2,1,0:T(8,128)(2,1)S(1)}, bf16[4,2,256,768]{3,2,1,0:T(8,128)(2,1)}, u32[]{:S(2)}, u32[]{:S(2)}) collective-permute-start(bf16[4,2,256,768]{3,2,1,0:T(8,128)(2,1)S(1)} %bitcast.65), channel_id=1, source_target_pairs={{0,16},{16,0},{1,17},{17,1},{2,18},{18,2},{3,19},{19,3},{4,20},{20... | collective-permute-start | bytes 9437192 | tf_op jit(solution)/shard_map/ppermute | solution.py:93
  469.4 25.8 %collective-permute-start.41 = (bf16[256,2048]{1,0:T(8,128)(2,1)}, bf16[256,2048]{1,0:T(8,128)(2,1)}, u32[]{:S(2)}, u32[]{:S(2)}) collective-permute-start(bf16[256,2048]{1,0:T(8,128)(2,1)} %get-tuple-element.116.refs_3_), channel_id=1, source_target_pairs={{0,4},{4,0},{8,12},{12,8},{1,5},{5,1},{9,13},{13,9},{2,6},{6,2},{1... | collective-permute-start | bytes 3145736 | tf_op jit(solution)/shard_map/ppermute | solution.py:93
  519.8 61.7 %collective-permute-start.48 = (bf16[512,2048]{1,0:T(8,128)(2,1)}, bf16[512,2048]{1,0:T(8,128)(2,1)S(1)}, u32[]{:S(2)}, u32[]{:S(2)}) collective-permute-start(bf16[512,2048]{1,0:T(8,128)(2,1)} %get-tuple-element.119.refs_13_), channel_id=1, source_target_pairs={{0,4},{4,0},{8,12},{12,8},{1,5},{5,1},{9,13},{13,9},{2,6},{6,2},{1... | collective-permute-start | bytes 6291464 | tf_op jit(solution)/shard_map/ppermute | solution.py:93
  533.4 49.4 %collective-permute-start.49 = (bf16[512,2048]{1,0:T(8,128)(2,1)}, bf16[512,2048]{1,0:T(8,128)(2,1)}, u32[]{:S(2)}, u32[]{:S(2)}) collective-permute-start(bf16[512,2048]{1,0:T(8,128)(2,1)} %get-tuple-element.121.refs_12_), channel_id=1, source_target_pairs={{0,8},{4,12},{8,0},{12,4},{1,9},{5,13},{9,1},{13,5},{2,10},{6,14},... | collective-permute-start | bytes 6291464 | tf_op jit(solution)/shard_map/ppermute | solution.py:93
  579.3 28.5 %collective-permute-start.42 = (bf16[512,2048]{1,0:T(8,128)(2,1)}, bf16[512,2048]{1,0:T(8,128)(2,1)S(1)}, u32[]{:S(2)}, u32[]{:S(2)}) collective-permute-start(bf16[512,2048]{1,0:T(8,128)(2,1)} %get-tuple-element.123.refs_1_), channel_id=1, source_target_pairs={{0,16},{16,0},{1,17},{17,1},{2,18},{18,2},{3,19},{19,3},{4,20},{20... | collective-permute-start | bytes 6291464 | tf_op jit(solution)/shard_map/ppermute | solution.py:93
  (94 other events, 706.8 us)
Sparse Core Ops, SparseCore 0:
  12.5 66.1 all-gather.8
  80.2 79.3 all-gather.10
  161.2 79.2 all-gather.12
  242.6 26.4 all-gather.14
  271.2 76.2 reduce-scatter.5
  390.1 73.6 reduce-scatter.3
  505.7 75.3 reduce-scatter.7
